TPU v7x, 32 devices: a whole 2x2x4 slice. The times are simulated.
32 devices in a mesh: dp: 4 (over y, x), mp: 8 (over z, core).
Axes of the slice: x: 2, y: 2, z: 4, core: 2. Of those that a mesh axis runs over, the one named last changes fastest.
Arguments:
- tokens: bfloat16 [1536, 2048], P('dp'), may hold values from -6 to 6
- cotangent: bfloat16 [1536, 2048], P('dp'), may hold values from -6 to 6
- norm_gains: float32 [2, 2048], replicated, may hold values from 0.1 to 1.9
- w_attn: bfloat16 [4, 2048, 2048], P(None, 'mp'), may hold values from -0.125 to 0.125
- w_in: bfloat16 [2, 2048, 5632], P(None, 'mp'), may hold values from -0.125 to 0.125
- w_down: bfloat16 [5632, 2048], P('mp'), may hold values from -0.078125 to 0.078125
- segments: int32 [4, 384], P('dp'), may hold values from 0 to 5, never falling along the last dimension, each value on 1 to 288 neighbouring positions
- owners: int32 [637], replicated, may hold values from 0 to 31, as said below
- master: float32 [1280, 1024], P(('dp', 'mp'))
- first_moment: float32 [1280, 1024], P(('dp', 'mp'))
- second_moment: float32 [1280, 1024], P(('dp', 'mp'))
Outputs:
- layer_out: bfloat16 [1536, 2048], P('dp')
- input_grad: float32 [1536, 2048], P('dp')
- new_master: float32 [1280, 1024], P(('dp', 'mp'))
- new_first: float32 [1280, 1024], P(('dp', 'mp'))
- new_second: float32 [1280, 1024], P(('dp', 'mp'))
Inputs may be any that keep to these rules, and one draw needn't show every extreme that they name: `segments`: segment numbers never fall along a row. `owners`: no device keeps more than 40 blocks, and some device keeps exactly 40.
All inputs are finite; a program needn't handle non-finite values.
Results may differ from a plain program's by a relative error of at most 0.014.
The roundings to bfloat16 on the way count: a program that leaves them out, or rounds other values in their place, can miss the bound.
Values may be sent and summed in bfloat16 or wider, within the bound.
No kernel may reach another device: no remote copies, remote signals or barrier semaphores. Data moves between devices by JAX's collectives and lax.ppermute only.
A program may use at most 320 MiB of HBM per device.

v0:
```python
import jax
import jax.numpy as jnp
from jax import lax
from jax.sharding import PartitionSpec as P

D = 2048
FF = 5632
HEADS = 16
HEAD_DIM = 128
RANK = 16
BLOCK = 1024
STEP = 5


dora_scale = 2.0
rope_base = 10000.0
norm_eps = 1e-05
column_eps = 1e-06
beta_one = 0.5
beta_two = 0.5
adam_eps = 1e-08
weight_decay = 0.01
rate_lower = 0.02
rate_upper = 0.1
rate_magnitude = 1.0
highest = lax.Precision.HIGHEST


def proj_dims():
    return [(D, D), (D, D), (D, D), (D, D), (D, FF), (D, FF), (FF, D)]


def unpack(flat):
    offset = 0
    lowers = []
    for inner, outer in proj_dims():
        lowers.append(flat[offset : offset + inner * RANK].reshape(inner, RANK))
        offset += inner * RANK
    uppers = []
    for inner, outer in proj_dims():
        uppers.append(flat[offset : offset + outer * RANK].reshape(outer, RANK))
        offset += outer * RANK
    magnitudes = []
    for inner, outer in proj_dims():
        magnitudes.append(flat[offset : offset + outer])
        offset += outer
    return (lowers, uppers, magnitudes)


def slot_positions(owners, capacity):
    order = jnp.arange(owners.shape[0], dtype=jnp.int32)
    same = (owners[:, None] == owners[None, :]) & (order[None, :] < order[:, None])
    ranks = jnp.sum(same.astype(jnp.int32), axis=1)
    return owners * capacity + ranks


def block_rates(block_ids):
    count_lower = RANK * (6 * D + FF) // BLOCK
    count_upper = RANK * (5 * D + 2 * FF) // BLOCK
    rates = jnp.where(block_ids < count_lower + count_upper, rate_upper, rate_magnitude)
    rates = jnp.where(block_ids < count_lower, rate_lower, rates)
    return jnp.where(block_ids < 0, 0.0, rates).astype(jnp.float32)


def adam_update(weight, grad, first, second, rates):
    first_new = beta_one * first + (1.0 - beta_one) * grad
    second_new = beta_two * second + (1.0 - beta_two) * grad * grad
    first_hat = first_new / (1.0 - beta_one**STEP)
    second_hat = second_new / (1.0 - beta_two**STEP)
    weight_new = weight - rates[:, None] * (
        first_hat / (jnp.sqrt(second_hat) + adam_eps) + weight_decay * weight
    )
    return (weight_new, first_new, second_new)


def rms_norm(values, gain):
    return values * lax.rsqrt(jnp.mean(values * values, axis=-1, keepdims=True) + norm_eps) * gain


def rms_back(values, grad, gain):
    inverse = lax.rsqrt(jnp.mean(values * values, axis=-1, keepdims=True) + norm_eps)
    scaled = grad * gain
    return inverse * (
        scaled - values * inverse * inverse * jnp.mean(scaled * values, axis=-1, keepdims=True)
    )


def segment_positions(row):
    order = jnp.arange(row.shape[0], dtype=jnp.int32)
    change = jnp.concatenate([jnp.ones((1,), dtype=bool), row[1:] != row[:-1]])
    starts = lax.cummax(jnp.where(change, order, 0), axis=0)
    return order - starts


def rotary_tables(positions):
    half = HEAD_DIM // 2
    freqs = rope_base ** (-(jnp.arange(half).astype(jnp.float32) * 2.0 / HEAD_DIM))
    angles = positions.astype(jnp.float32)[:, None] * freqs[None, :]
    return (jnp.cos(angles)[:, None, :], jnp.sin(angles)[:, None, :])


def rotate(values, cosine, sine):
    half = values.shape[-1] // 2
    first_half = values[..., :half]
    second_half = values[..., half:]
    return jnp.concatenate(
        [first_half * cosine - second_half * sine, second_half * cosine + first_half * sine],
        axis=-1,
    )


def unrotate(values, cosine, sine):
    half = values.shape[-1] // 2
    first_half = values[..., :half]
    second_half = values[..., half:]
    return jnp.concatenate(
        [first_half * cosine + second_half * sine, second_half * cosine - first_half * sine],
        axis=-1,
    )


def body(
    tokens,
    cotangent,
    norm_gains,
    w_attn,
    w_in,
    w_down,
    segments,
    owners,
    master,
    first_moment,
    second_moment,
):
    group_rows = tokens.shape[0]
    model_size = lax.axis_size("mp")
    model_index = lax.axis_index("mp")
    share = group_rows // model_size
    share_start = model_index * share
    capacity = master.shape[0]
    everyone = lax.axis_size(("dp", "mp"))
    score_scale = HEAD_DIM ** (-0.5)
    widths = [outer for inner, outer in proj_dims()]
    slot_index = slot_positions(owners, capacity)
    copies = lax.all_gather(master.astype(jnp.bfloat16), ("dp", "mp"), axis=0, tiled=True)
    lowers, uppers, magnitudes = unpack(jnp.take(copies, slot_index, axis=0).reshape(-1))
    frozen = [w_attn[0], w_attn[1], w_attn[2], w_attn[3], w_in[0], w_in[1], w_down]
    lower_local = []
    combined = []
    square_parts = []
    for index in range(7):
        rows_here = frozen[index].shape[0]
        piece = lax.dynamic_slice_in_dim(lowers[index], model_index * rows_here, rows_here, 0)
        lower_local.append(piece)
        joined = frozen[index].astype(jnp.float32) + dora_scale * jnp.dot(
            piece.astype(jnp.float32), uppers[index].astype(jnp.float32).T, precision=highest
        )
        combined.append(joined)
        square_parts.append(jnp.sum(joined * joined, axis=0))

    def rows_of(values):
        return lax.dynamic_slice_in_dim(values, share_start, share, 0)

    def split_parts(values, indices, axis):
        pieces = []
        offset = 0
        for index in indices:
            pieces.append(lax.slice_in_dim(values, offset, offset + widths[index], axis=axis))
            offset += widths[index]
        return pieces

    norms = [None] * 7
    mixed_share = [None] * 7
    low_share = [None] * 7
    mixed_full = [None] * 7
    grads = [None] * 7

    def set_scales(indices):
        summed = lax.psum(jnp.concatenate([square_parts[index] for index in indices]), "mp")
        squares = split_parts(summed, indices, 0)
        for index, value in zip(indices, squares):
            norms[index] = jnp.sqrt(value + column_eps)

    def scale(index):
        return magnitudes[index].astype(jnp.float32) / norms[index]

    def local_partials(inputs_local, indices):
        mixed_list = []
        low_list = []
        for index in indices:
            low_part = jnp.dot(inputs_local, lower_local[index], preferred_element_type=jnp.float32)
            mixed = jnp.dot(
                inputs_local, frozen[index], preferred_element_type=jnp.float32
            ) + dora_scale * jnp.dot(
                low_part, uppers[index].astype(jnp.float32).T, precision=highest
            )
            mixed_list.append(mixed)
            low_list.append(low_part)
        return (
            inputs_local,
            jnp.concatenate(mixed_list, axis=1),
            jnp.concatenate(low_list, axis=1),
        )

    def group_partials(inputs_b, indices):
        rows_here = frozen[indices[0]].shape[0]
        inputs_local = lax.dynamic_slice_in_dim(inputs_b, model_index * rows_here, rows_here, 1)
        return local_partials(inputs_local, indices)

    def finish(indices, local_mixed, local_low):
        summed_mixed, summed_low = lax.psum((local_mixed, local_low), "mp")
        pieces = split_parts(summed_mixed, indices, 1)
        for position, index in enumerate(indices):
            mixed_full[index] = pieces[position]
            mixed_share[index] = rows_of(pieces[position])
            low_share[index] = rows_of(summed_low[:, position * RANK : (position + 1) * RANK])
        return pieces

    def gather_inputs(local):
        return lax.all_gather(local, "mp", axis=1, tiled=True)

    xf = tokens.astype(jnp.float32)
    row = segments[0]
    cosine, sine = rotary_tables(segment_positions(row))
    order = jnp.arange(group_rows)
    allowed = (row[:, None] == row[None, :]) & (order[None, :] <= order[:, None])
    features = rms_norm(xf, norm_gains[0]).astype(jnp.bfloat16)
    first_local, first_mixed, first_low = group_partials(features, (0, 1, 2))
    set_scales((0, 1, 2))
    summed_mixed, summed_low = lax.psum((first_mixed, first_low), "mp")
    pieces = split_parts(summed_mixed, (0, 1, 2), 1)
    heads_in = []
    for index in range(3):
        mixed_full[index] = pieces[index]
        mixed_share[index] = rows_of(pieces[index])
        low_share[index] = rows_of(summed_low[:, index * RANK : (index + 1) * RANK])
        projected = (pieces[index] * scale(index)).reshape(group_rows, HEADS, HEAD_DIM)
        if index < 2:
            projected = rotate(projected, cosine, sine)
        heads_in.append(projected.astype(jnp.bfloat16))
    query_b, key_b, value_b = heads_in

    def attention_scores(query_h, key_h):
        scores = (
            jnp.einsum("thd,shd->hts", query_h, key_h, preferred_element_type=jnp.float32)
            * score_scale
        )
        return jnp.where(allowed[None], scores, -1e30)

    scores = attention_scores(query_b, key_b)
    top = jnp.max(scores, axis=-1, keepdims=True)
    expd = jnp.exp(scores - top)
    total = jnp.sum(expd, axis=-1, keepdims=True)
    probs = (expd / total).astype(jnp.bfloat16)
    attended_h = jnp.einsum("hts,shd->thd", probs, value_b, preferred_element_type=jnp.float32)
    attended_h, log_total = (attended_h, top + jnp.log(total))
    attended = attended_h.reshape(group_rows, D).astype(jnp.bfloat16)
    out_local, out_mixed, out_low = group_partials(attended, (3,))
    set_scales((3,))
    x_two = xf + finish((3,), out_mixed, out_low)[0] * scale(3)
    second_features = rms_norm(x_two, norm_gains[1]).astype(jnp.bfloat16)
    ffn_local, ffn_mixed, ffn_low = group_partials(second_features, (4, 5))
    set_scales((4, 5))
    gate_pre, up_pre = finish((4, 5), ffn_mixed, ffn_low)
    gate = gate_pre * scale(4)
    upward = up_pre * scale(5)
    sigmoid_gate = jax.nn.sigmoid(gate)
    act = (gate * sigmoid_gate * upward).astype(jnp.bfloat16)
    down_local, down_mixed, down_low = group_partials(act, (6,))
    set_scales((6,))
    down_pre = finish((6,), down_mixed, down_low)[0]
    layer_out = (x_two + down_pre * scale(6)).astype(jnp.bfloat16)

    def whole_dot(index, grad):
        return jnp.sum(grad * mixed_full[index], axis=0)

    def project_back(index, grad, inputs_local, group_dot):
        norm = norms[index]
        magnitude = magnitudes[index].astype(jnp.float32)
        grad_b = (grad * (magnitude / norm)).astype(jnp.bfloat16)
        share_dot = jnp.sum(rows_of(grad) * mixed_share[index], axis=0)
        grad_full = combined[index] * (-group_dot * magnitude / (norm * norm * norm))[None, :]
        upper_f = uppers[index].astype(jnp.float32)
        lower_f = lower_local[index].astype(jnp.float32)
        through = dora_scale * jnp.dot(grad_b, uppers[index], preferred_element_type=jnp.float32)
        grad_lower = jnp.dot(
            inputs_local.astype(jnp.float32).T, through, precision=highest
        ) + dora_scale * jnp.dot(grad_full, upper_f, precision=highest)
        grad_upper = dora_scale * jnp.dot(
            rows_of(grad_b).astype(jnp.float32).T, low_share[index], precision=highest
        ) + dora_scale * jnp.dot(grad_full.T, lower_f, precision=highest)
        grads[index] = (grad_lower, grad_upper, share_dot / norm)
        return jnp.dot(grad_b, frozen[index].T, preferred_element_type=jnp.float32) + jnp.dot(
            through, lower_f.T, precision=highest
        )

    grad_out = cotangent.astype(jnp.float32)
    grad_act = gather_inputs(project_back(6, grad_out, down_local, whole_dot(6, grad_out)))
    grad_gate = grad_act * upward * sigmoid_gate * (1.0 + gate * (1.0 - sigmoid_gate))
    grad_up = grad_act * gate * sigmoid_gate
    ffn_back = project_back(4, grad_gate, ffn_local, whole_dot(4, grad_gate)) + project_back(
        5, grad_up, ffn_local, whole_dot(5, grad_up)
    )
    grad_two = grad_out + rms_back(x_two, gather_inputs(ffn_back), norm_gains[1])
    grad_att = gather_inputs(project_back(3, grad_two, out_local, whole_dot(3, grad_two)))
    grad_att = grad_att.astype(jnp.bfloat16).reshape(group_rows, HEADS, HEAD_DIM)
    weights = jnp.exp(attention_scores(query_b, key_b) - log_total)
    weights_b = weights.astype(jnp.bfloat16)
    grad_weights = jnp.einsum("thd,shd->hts", grad_att, value_b, preferred_element_type=jnp.float32)
    grad_value = jnp.einsum("hts,thd->shd", weights_b, grad_att, preferred_element_type=jnp.float32)
    centred = jnp.sum(weights * grad_weights, axis=-1, keepdims=True)
    grad_scores = (weights * (grad_weights - centred)).astype(jnp.bfloat16)
    grad_query = (
        jnp.einsum("hts,shd->thd", grad_scores, key_b, preferred_element_type=jnp.float32)
        * score_scale
    )
    grad_key = (
        jnp.einsum("hts,thd->shd", grad_scores, query_b, preferred_element_type=jnp.float32)
        * score_scale
    )
    grad_query, grad_key, grad_value = (
        unrotate(grad_query, cosine, sine),
        unrotate(grad_key, cosine, sine),
        grad_value,
    )
    incoming = [
        grad_query.reshape(group_rows, D),
        grad_key.reshape(group_rows, D),
        grad_value.reshape(group_rows, D),
    ]
    group_dots = [whole_dot(index, incoming[index]) for index in range(3)]
    first_back = project_back(0, incoming[0], first_local, group_dots[0])
    first_back = first_back + project_back(1, incoming[1], first_local, group_dots[1])
    first_back = first_back + project_back(2, incoming[2], first_local, group_dots[2])
    input_grad = grad_two + rms_back(xf, gather_inputs(first_back), norm_gains[0])
    pieces = []
    for index in range(7):
        rows_total = proj_dims()[index][0]
        grad_lower = grads[index][0]
        placed = lax.dynamic_update_slice_in_dim(
            jnp.zeros((rows_total, RANK), jnp.float32),
            grad_lower,
            model_index * grad_lower.shape[0],
            0,
        )
        pieces.append(placed.reshape(-1))
    for index in range(7):
        pieces.append(grads[index][1].reshape(-1))
    for index in range(7):
        pieces.append(grads[index][2])
    blocks = jnp.concatenate(pieces).reshape(-1, BLOCK)
    buffer = jnp.zeros((capacity * everyone, BLOCK), jnp.float32).at[slot_index].set(blocks)
    owned = lax.psum_scatter(buffer, ("dp", "mp"), scatter_dimension=0, tiled=True)
    slot_block = (
        jnp.full((capacity * everyone,), -1, jnp.int32)
        .at[slot_index]
        .set(jnp.arange(blocks.shape[0], dtype=jnp.int32))
    )
    local_blocks = lax.dynamic_slice_in_dim(
        slot_block, lax.axis_index(("dp", "mp")) * capacity, capacity, 0
    )
    new_master, new_first, new_second = adam_update(
        master, owned, first_moment, second_moment, block_rates(local_blocks)
    )
    return (layer_out, input_grad, new_master, new_first, new_second)


def solution(mesh):
    return jax.shard_map(
        body,
        mesh=mesh,
        in_specs=(
            P("dp", None),
            P("dp", None),
            P(),
            P(None, "mp", None),
            P(None, "mp", None),
            P("mp", None),
            P("dp", None),
            P(),
            P(("dp", "mp"), None),
            P(("dp", "mp"), None),
            P(("dp", "mp"), None),
        ),
        out_specs=(
            P("dp", None),
            P("dp", None),
            P(("dp", "mp"), None),
            P(("dp", "mp"), None),
            P(("dp", "mp"), None),
        ),
        check_vma=False,
    )
```

profile of v0, /device:TPU:1, one launch (start us, length us, event | category | flops | bytes accessed | tf_op | source)
XLA Modules:
  0.0 1554.8 jit_solution(11304795512300467945)
XLA Ops:
  23.2 48.9 %all-gather.6.cloned.1.call-done = bf16[1280,1024]{1,0:T(8,128)(2,1)} async-done(((bf16[40,1024]{1,0:T(8,128)(2,1)}), bf16[1280,1024]{1,0:T(8,128)(2,1)}) %all-gather.6.cloned.1.call-update) | async-done | bytes 2621456 | tf_op jit(solution)/shard_map/all_gather | solution.py:145
  72.1 6.0 gather_fusion
  91.0 3.7 multiply_reduce_fusion.16
  103.3 5.6 multiply_reduce_fusion.4
  108.9 5.5 multiply_reduce_fusion.5
  115.1 4.0 multiply_reduce_fusion.13
  119.2 3.4 multiply_add_fusion.8
  129.9 8.5 pad_maximum_fusion.1
  142.4 37.2 %all-reduce.18.cloned.1.call-done = (f32[11264]{0:T(1024)}, f32[6144]{0:T(1024)}, f32[2048]{0:T(1024)}) async-done(((f32[11264]{0:T(1024)}, f32[6144]{0:T(1024)}, f32[2048]{0:T(1024)}), (f32[11264]{0:T(1024)}, f32[6144]{0:T(1024)}, f32[2048]{0:T(1024)})) %all-reduce.18.cloned.1.call-update) | async-done | bytes 77840 | tf_op jit(solution)/shard_map/psum | solution.py:179
  180.3 198.6 %all-reduce.10.cloned.1.call-done = f32[384,6144]{1,0:T(8,128)} async-done(((f32[384,6144]{1,0:T(8,128)}), f32[384,6144]{1,0:T(8,128)}) %all-reduce.10.cloned.1.call-update) | async-done | bytes 9437200 | tf_op jit(solution)/shard_map/psum | solution.py:230
  378.9 10.6 fusion.277
  395.7 4.0 subtract_convert_fusion.1
  417.0 76.0 %all-reduce.12.cloned.1.call-done = f32[384,2048]{1,0:T(8,128)} async-done(((f32[384,2048]{1,0:T(8,128)}), f32[384,2048]{1,0:T(8,128)}) %all-reduce.12.cloned.1.call-update) | async-done | bytes 3145744 | tf_op jit(solution)/shard_map/psum | solution.py:211
  499.9 3.9 convolution_multiply_fusion.1
  505.2 3.8 convolution_multiply_fusion
  512.2 6.7 pad_maximum_fusion
  525.8 6.3 multiply_reduce_fusion.3
  534.2 327.8 %all-reduce.14.cloned.1.call-done = f32[384,11264]{1,0:T(8,128)} async-done(((f32[384,11264]{1,0:T(8,128)}), f32[384,11264]{1,0:T(8,128)}) %all-reduce.14.cloned.1.call-update) | async-done | bytes 17301520 | tf_op jit(solution)/shard_map/psum | solution.py:211
  862.1 18.7 %add_divide_fusion = (f32[384,5632]{1,0:T(8,128)}, f32[384,5632]{1,0:T(8,128)}, f32[384,5632]{1,0:T(8,128)}, f32[384,5632]{1,0:T(8,128)}, f32[384,5632]{1,0:T(8,128)}) fusion(f32[5632]{0:T(1024)} %get-tuple-element.60, f32[384,11264]{1,0:T(8,128)} %all-reduce.14.cloned.1.call-done, f32[5632]{0:T(1024)} %get-tuple-element.61), kind=kLoop, calls=%fused_computation.21 | loop fusion | flops 10813440 | bytes 60600320 | tf_op jit(solution)/shard_map/div | solution.py:267
  890.8 55.0 %all-reduce.16.cloned.1.call-done = (f32[2048]{0:T(1024)}, f32[384,16]{0,1:T(8,128)}, f32[384,32]{0,1:T(8,128)}, f32[384,16]{0,1:T(8,128)}) async-done(((f32[2048]{0:T(1024)}, f32[384,16]{0,1:T(8,128)}, f32[384,32]{0,1:T(8,128)}, f32[384,16]{0,1:T(8,128)}), (f32[2048]{0:T(1024)}, f32[384,16]{0,1:T(8,128)}, f32[384,32]{0,1:T(8,128)}, f32[384,16]{0,1:T(8,128)})) %all-reduce.16.cloned.1.call-update) | async-done | bytes 106512 | tf_op jit(solution)/shard_map/psum | solution.py:179
  954.2 86.1 %all-gather.8.cloned.1.call-done = f32[384,5632]{0,1:T(8,128)} async-done(((f32[384,704]{0,1:T(8,128)}), f32[384,5632]{0,1:T(8,128)}) %all-gather.8.cloned.1.call-update) | async-done | bytes 8650768 | tf_op jit(solution)/shard_map/all_gather | solution.py:220
  1040.3 9.5 copy.117
  1049.7 19.4 %multiply_reduce_fusion.1 = (f32[5632]{0:T(1024)S(1)}, f32[5632]{0:T(1024)S(1)}, f32[384,5632]{1,0:T(8,128)S(1)}, f32[384,5632]{1,0:T(8,128)}) fusion(f32[384,11264]{1,0:T(8,128)} %all-reduce.14.cloned.1.call-done, f32[384,5632]{1,0:T(8,128)} %get-tuple-element.27, f32[384,5632]{1,0:T(8,128)} %copy.117, f32[384,5632]{1,0:T(8,128)} %get-tuple-element.32), kind=kLoop, calls=%fused_computation.15 | loop fusion | flops 32429056 | bytes 60600320 | tf_op jit(solution)/shard_map/reduce_sum | solution.py:275
  1072.5 5.8 multiply_convert_fusion.1
  1078.4 4.7 fusion.24
  1090.8 3.6 convert_element_type.289
  1099.8 21.1 %all-reduce.20.cloned.1.call-done = (f32[384,2048]{1,0:T(8,128)}, f32[384,48]{0,1:T(8,128)}) async-done(((f32[384,2048]{1,0:T(8,128)}, f32[384,48]{0,1:T(8,128)}), (f32[384,2048]{1,0:T(8,128)}, f32[384,48]{0,1:T(8,128)})) %all-reduce.20.cloned.1.call-update) | async-done | bytes 3219472 | tf_op jit(solution)/shard_map/psum | solution.py:211
  1127.9 5.8 fusion.5
  1133.7 3.7 fusion.4
  1137.5 23.4 %all-gather.10.cloned.1.call-done = f32[384,2048]{1,0:T(8,128)} async-done(((f32[384,256]{1,0:T(8,128)}), f32[384,2048]{1,0:T(8,128)}) %all-gather.10.cloned.1.call-update) | async-done | bytes 3145744 | tf_op jit(solution)/shard_map/all_gather | solution.py:220
  1160.8 7.4 multiply_reduce_fusion.11
  1188.1 5.7 fusion.123
  1198.2 5.7 fusion.117
  1209.7 4.8 fusion.45
  1215.8 5.4 fusion.87
  1230.7 11.1 multiply_reduce_fusion
  1241.8 11.3 multiply_convert_fusion
  1253.1 4.9 multiply_bitcast_fusion
  1258.0 4.9 multiply_bitcast_fusion.1
  1263.0 4.3 fusion.23
  1270.8 4.0 multiply_add_fusion.3
  1297.0 4.0 copy.156
  1308.7 5.3 multiply_reduce_fusion.8
  1391.9 3.7 reshape.567
  1395.6 9.2 scatter_custom_fusion.1
  1404.9 4.2 scatter_custom_fusion
  1412.2 4.6 multiply_add_fusion.1
  1416.7 129.3 %reduce-scatter.2.cloned.1.call-done = f32[40,1024]{1,0:T(8,128)} async-done(((f32[1280,1024]{1,0:T(8,128)}), f32[40,1024]{1,0:T(8,128)}) %reduce-scatter.2.cloned.1.call-update) | async-done | bytes 163856 | tf_op jit(solution)/shard_map/reduce_scatter | solution.py:353
  (614 shorter events, 291.2 us)
Async XLA Ops:
  7.2 64.9 %all-gather.6.cloned.1.call-start = ((), (), s32[]{:S(2)}) async-start(), calls=%async_computation.1 | async-start | bytes 2703360 | tf_op jit(solution)/shard_map/all_gather | solution.py:145
  8.8 170.7 %all-reduce.18.cloned.1.call-start = ((), (), s32[]{:S(2)}) async-start(), calls=%async_computation.11 | async-start | bytes 155648 | tf_op jit(solution)/shard_map/psum | solution.py:179
  16.4 73.8 %copy-start.18 = (bf16[384,256]{1,0:T(8,128)(2,1)}, bf16[384,256]{1,0:T(8,128)(2,1)S(1)}, u32[]{:S(2)}) copy-start(bf16[384,256]{1,0:T(8,128)(2,1)S(1)} %fusion.166) | copy-start | bytes 589828
  90.2 32.3 %copy-start.37 = (bf16[2048,16]{1,0:T(8,128)(2,1)}, bf16[2048,16]{1,0:T(8,128)(2,1)S(1)}, u32[]{:S(2)}) copy-start(bf16[2048,16]{1,0:T(8,128)(2,1)S(1)} %reshape.504) | copy-start | bytes 196612
  97.1 11.8 copy-start.7
  100.8 984.9 %copy-start.5 = (bf16[5632,16]{1,0:T(8,128)(2,1)}, bf16[5632,16]{1,0:T(8,128)(2,1)S(1)}, u32[]{:S(2)}) copy-start(bf16[5632,16]{1,0:T(8,128)(2,1)S(1)} %reshape.515) | copy-start | bytes 540676
  129.8 249.1 %all-reduce.10.cloned.1.call-start = ((), (), s32[]{:S(2)}) async-start(), calls=%async_computation.2 | async-start | bytes 18874368 | tf_op jit(solution)/shard_map/psum | solution.py:230
  138.4 354.6 %all-reduce.12.cloned.1.call-start = ((), (), s32[]{:S(2)}) async-start(), calls=%async_computation.3 | async-start | bytes 6291456 | tf_op jit(solution)/shard_map/psum | solution.py:211
  140.0 265.0 %copy-start.62 = (pred[384,384]{0,1:T(8,128)(4,1)}, pred[384,384]{0,1:T(8,128)(4,1)S(1)}, u32[]{:S(2)}) copy-start(pred[384,384]{0,1:T(8,128)(4,1)S(1)} %fusion.160) | copy-start | bytes 442372
  140.8 254.9 %copy-start.67 = (f32[384,64]{1,0:T(8,128)}, f32[384,64]{1,0:T(8,128)S(1)}, u32[]{:S(2)}) copy-start(f32[384,64]{1,0:T(8,128)S(1)} %get-tuple-element.104) | copy-start | bytes 294916
  140.8 254.9 %copy-start.69 = (f32[384,64]{1,0:T(8,128)}, f32[384,64]{1,0:T(8,128)S(1)}, u32[]{:S(2)}) copy-start(f32[384,64]{1,0:T(8,128)S(1)} %get-tuple-element.105) | copy-start | bytes 294916
  142.4 247.1 %copy-start.149 = (f32[1,8,2,128]{3,2,1,0:T(2,128)}, f32[1,8,2,128]{3,2,1,0:T(2,128)S(1)}, u32[]{:S(2)}) copy-start(f32[1,8,2,128]{3,2,1,0:T(2,128)S(1)} %get-tuple-element.63) | copy-start | bytes 24580
  142.4 247.1 %copy-start.151 = (f32[1,8,2,128]{3,2,1,0:T(2,128)}, f32[1,8,2,128]{3,2,1,0:T(2,128)S(1)}, u32[]{:S(2)}) copy-start(f32[1,8,2,128]{3,2,1,0:T(2,128)S(1)} %get-tuple-element.64) | copy-start | bytes 24580
  142.4 247.1 %copy-start.153 = (f32[1,8,2,128]{3,2,1,0:T(2,128)}, f32[1,8,2,128]{3,2,1,0:T(2,128)S(1)}, u32[]{:S(2)}) copy-start(f32[1,8,2,128]{3,2,1,0:T(2,128)S(1)} %get-tuple-element.65) | copy-start | bytes 24580
  180.3 209.2 %copy-start.132 = (f32[2048]{0:T(1024)}, f32[2048]{0:T(1024)S(1)}, u32[]{:S(2)}) copy-start(f32[2048]{0:T(1024)S(1)} %get-tuple-element.99) | copy-start | bytes 24580
  180.3 209.2 %copy-start.134 = (f32[2048]{0:T(1024)}, f32[2048]{0:T(1024)S(1)}, u32[]{:S(2)}) copy-start(f32[2048]{0:T(1024)S(1)} %get-tuple-element.101) | copy-start | bytes 24580
  180.3 209.2 %copy-start.136 = (f32[2048]{0:T(1024)}, f32[2048]{0:T(1024)S(1)}, u32[]{:S(2)}) copy-start(f32[2048]{0:T(1024)S(1)} %get-tuple-element.100) | copy-start | bytes 24580
  416.3 76.8 %copy-start.1 = (bf16[384,2048]{1,0:T(8,128)(2,1)S(1)}, bf16[384,2048]{1,0:T(8,128)(2,1)}, u32[]{:S(2)}) copy-start(bf16[384,2048]{1,0:T(8,128)(2,1)} %param.11) | copy-start | bytes 4718596
  416.3 445.8 %all-reduce.14.cloned.1.call-start = ((), (), s32[]{:S(2)}) async-start(), calls=%async_computation.4 | async-start | bytes 34603008 | tf_op jit(solution)/shard_map/psum | solution.py:211
  496.5 12.6 copy-start.56
  525.8 422.7 %copy-start.35 = (bf16[2048,16]{1,0:T(8,128)(2,1)}, bf16[2048,16]{1,0:T(8,128)(2,1)S(1)}, u32[]{:S(2)}) copy-start(bf16[2048,16]{1,0:T(8,128)(2,1)S(1)} %reshape.519) | copy-start | bytes 196612
  890.2 55.6 %all-reduce.16.cloned.1.call-start = ((), (), s32[]{:S(2)}) async-start(), calls=%async_computation.10 | async-start | bytes 212992 | tf_op jit(solution)/shard_map/psum | solution.py:179
  890.8 149.5 %all-gather.8.cloned.1.call-start = ((), (), s32[]{:S(2)}) async-start(), calls=%async_computation.5 | async-start | bytes 9732096 | tf_op jit(solution)/shard_map/all_gather | solution.py:220
  953.4 167.5 %all-reduce.20.cloned.1.call-start = ((), (), s32[]{:S(2)}) async-start(), calls=%async_computation.12 | async-start | bytes 6438912 | tf_op jit(solution)/shard_map/psum | solution.py:211
  954.1 206.7 %all-gather.10.cloned.1.call-start = ((), (), s32[]{:S(2)}) async-start(), calls=%async_computation.6 | async-start | bytes 3538944 | tf_op jit(solution)/shard_map/all_gather | solution.py:220
  1049.7 19.4 %copy-start.119 = (f32[5632]{0:T(1024)S(1)}, f32[5632]{0:T(1024)}, u32[]{:S(2)}) copy-start(f32[5632]{0:T(1024)} %get-tuple-element.60) | copy-start | bytes 67588
  1072.5 14.5 copy-start.15
  1090.5 138.2 %all-gather.12.cloned.1.call-start = ((), (), s32[]{:S(2)}) async-start(), calls=%async_computation.7 | async-start | bytes 1769472 | tf_op jit(solution)/shard_map/all_gather | solution.py:220
  1090.8 42.9 %slice-start.3 = ((s8[5767168]{0:T(1024)(128)(4,1)}), s8[1572864]{0:T(1024)(128)(4,1)S(1)}, s32[]{:S(2)}) async-start(s8[5767168]{0:T(1024)(128)(4,1)} %bitcast.222), calls=%async_computation.16 | async-start | bytes 3145728
  1094.4 32.7 %copy-start.91 = (f32[11264]{0:T(1024)S(1)}, f32[11264]{0:T(1024)}, u32[]{:S(2)}) copy-start(f32[11264]{0:T(1024)} %get-tuple-element.14) | copy-start | bytes 135172
  1133.7 27.1 %copy-start.139 = (f32[2048]{0:T(1024)S(1)}, f32[2048]{0:T(1024)}, u32[]{:S(2)}) copy-start(f32[2048]{0:T(1024)} %copy-done.138) | copy-start | bytes 24580
  1137.5 30.8 %copy-start.17 = (bf16[384,2048]{1,0:T(8,128)(2,1)S(1)}, bf16[384,2048]{1,0:T(8,128)(2,1)}, u32[]{:S(2)}) copy-start(bf16[384,2048]{1,0:T(8,128)(2,1)} %param.12) | copy-start | bytes 4718596
  1137.5 30.8 %copy-start.171 = (f32[384]{0:T(512)S(1)}, f32[384]{0:T(512)}, u32[]{:S(2)}) copy-start(f32[384]{0:T(512)} %copy-done.170) | copy-start | bytes 4612
  1176.1 233.1 %all-gather.14.cloned.1.call-start = ((), (), s32[]{:S(2)}) async-start(), calls=%async_computation.8 | async-start | bytes 3538944 | tf_op jit(solution)/shard_map/all_gather | solution.py:220
  1230.6 11.1 copy-start.33
  1241.8 16.2 %copy-start.30 = (bf16[384,16,64]{2,0,1:T(8,128)(2,1)S(1)}, bf16[384,16,64]{2,0,1:T(8,128)(2,1)}, u32[]{:S(2)}) copy-start(bf16[384,16,64]{2,0,1:T(8,128)(2,1)} %copy-done.29) | copy-start | bytes 2359300
  1303.5 13.5 copy-start.64
  1314.6 14.2 copy-start.143
  1361.5 10.5 copy-start.81
  1361.5 11.1 copy-start.73
  1362.2 11.2 copy-start.84
  1363.6 10.4 copy-start.83
  1367.3 178.8 %reduce-scatter.2.cloned.1.call-start = ((), (), s32[]{:S(2)}) async-start(), calls=%async_computation.9 | async-start | bytes 5406720 | tf_op jit(solution)/shard_map/reduce_scatter | solution.py:353
  1379.5 11.8 copy-start.148
  1379.5 11.8 copy-start.158
  1412.2 133.9 %copy-start.79 = (f32[40,1024]{1,0:T(8,128)S(1)}, f32[40,1024]{1,0:T(8,128)}, u32[]{:S(2)}) copy-start(f32[40,1024]{1,0:T(8,128)} %param.19) | copy-start | bytes 491524
  1412.2 133.9 %copy-start.123 = (f32[40,1024]{1,0:T(8,128)S(1)}, f32[40,1024]{1,0:T(8,128)}, u32[]{:S(2)}) copy-start(f32[40,1024]{1,0:T(8,128)} %param.20) | copy-start | bytes 491524
  1412.2 133.9 %copy-start.124 = (f32[40,1024]{1,0:T(8,128)S(1)}, f32[40,1024]{1,0:T(8,128)}, u32[]{:S(2)}) copy-start(f32[40,1024]{1,0:T(8,128)} %param.21) | copy-start | bytes 491524
  (147 other events, 734.1 us)
Sparse Core Ops, SparseCore 0:
  11.4 60.6 all-gather.5
  129.9 49.5 all-reduce.17
  182.0 196.7 all-reduce.9
  416.4 76.5 all-reduce.11
  519.0 343.0 all-reduce.13
  894.1 51.6 all-reduce.15
  953.5 86.7 all-gather.7
  1043.3 77.4 all-reduce.19
  1122.5 38.2 all-gather.9
  1176.2 26.0 all-gather.11
  1367.4 37.1 all-gather.13
  1406.8 139.1 reduce-scatter.1
where the time goes:
time: 1580 us; the launch traced here: 1550 us
  waiting for transfers between devices  1000 us (63%)
  matrix products  218 us (14%)
  other arithmetic  167 us (11%)
  local copies, waits for them, and re-layouts  148 us (9%)
  between operations  16.7 us (1%)
    psum x3, waiting for transfers between devices, finish(): summed_mixed, summed_low = lax.psum((local_mixed, local_low), 'mp')  425 us
    psum x1, waiting for transfers between devices, body(): summed_mixed, summed_low = lax.psum((first_mixed, first_low), 'mp')  199 us
    reduce_scatter x1, waiting for transfers between devices, body(): lax.psum_scatter(buffer, ('dp', 'mp'), scatter_dimension=0, tiled=True)  129 us
    all_gather x4, waiting for transfers between devices, gather_inputs(): return lax.all_gather(local, 'mp', axis=1, tiled=True)  109 us
    psum x2, waiting for transfers between devices, set_scales(): lax.psum(jnp.concatenate([square_parts[index] for index in indices]), 'mp')  92.1 us
    all_gather x1, waiting for transfers between devices, body(): lax.all_gather(master.astype(jnp.bfloat16), ('dp', 'mp'), axis=0, tiled=T...  48.9 us
  transfers between devices with their start and end apart: 12, of which 10 were waited for; matrix products, arithmetic and copies ran while one was open for 14% of the time, Pallas kernels for 0%

commit v1 on v0

--- a/solution.py
+++ b/solution.py
@@ -1,5 +1,6 @@
 import jax
 import jax.numpy as jnp
+import numpy as np
 from jax import lax
 from jax.sharding import PartitionSpec as P
 
@@ -365,9 +366,436 @@
     return (layer_out, input_grad, new_master, new_first, new_second)
 
 
+def swap_halves(values):
+    half = values.shape[-1] // 2
+    return jnp.concatenate([values[..., half:], values[..., :half]], axis=-1)
+
+
+def dot_t(left, right, **kwargs):
+    return lax.dot_general(
+        left, right, (((1,), (1,)), ((), ())), preferred_element_type=jnp.float32, **kwargs
+    )
+
+
+def dot_first(left, right, **kwargs):
+    return lax.dot_general(
+        left, right, (((0,), (0,)), ((), ())), preferred_element_type=jnp.float32, **kwargs
+    )
+
+
+def dot(left, right, **kwargs):
+    return jnp.dot(left, right, preferred_element_type=jnp.float32, **kwargs)
+
+
+def wide(left, right):
+    return dot(left.astype(jnp.float32), right.astype(jnp.float32), precision=highest)
+
+
+def wide_t(left, right):
+    return dot_t(left.astype(jnp.float32), right.astype(jnp.float32), precision=highest)
+
+
+def wide_first(left, right):
+    return dot_first(left.astype(jnp.float32), right.astype(jnp.float32), precision=highest)
+
+
+def block_order():
+    rows = lax.broadcasted_iota(jnp.int32, (BLOCK, BLOCK), 0)
+    cols = lax.broadcasted_iota(jnp.int32, (BLOCK, BLOCK), 1)
+    return (cols == (rows % RANK) * (BLOCK // RANK) + rows // RANK).astype(jnp.bfloat16)
+
+
+def fast_body(
+    tokens,
+    cotangent,
+    norm_gains,
+    w_attn,
+    w_in,
+    w_down,
+    segments,
+    owners,
+    master,
+    first_moment,
+    second_moment,
+):
+    group_rows = tokens.shape[0]
+    n_mp = lax.axis_size("mp")
+    n_dp = lax.axis_size("dp")
+    n_z = n_mp // 2
+    mi = lax.axis_index("mp")
+    di = lax.axis_index("dp")
+    core = mi % 2
+    zi = mi // 2
+    share = group_rows // n_mp
+    capacity = master.shape[0]
+    n_blocks = owners.shape[0]
+    n_heads = HEADS // n_mp
+    width_a = D // n_mp
+    width_f = FF // n_mp
+    score_scale = HEAD_DIM ** (-0.5)
+    f32 = jnp.float32
+    bf16 = jnp.bfloat16
+
+    def mp_swap(values, step):
+        return lax.ppermute(values, "mp", [(i, i ^ step) for i in range(n_mp)])
+
+    def dp_swap(values, step):
+        return lax.ppermute(values, "dp", [(i, i ^ step) for i in range(n_dp)])
+
+    def plane(values):
+        half = values.shape[0] // 2
+        a, b = values[:half], values[half:]
+        ax, by = dp_swap(a, 1), dp_swap(b, 2)
+        ay, bx = dp_swap(a, 2), dp_swap(b, 1)
+        axy, bxy = dp_swap(ax, 2), dp_swap(by, 1)
+        return jnp.stack([jnp.stack([a, ax, ay, axy]), jnp.stack([b, bx, by, bxy])], axis=1)
+
+    def scatter_rows(values):
+        rows = values.shape[0] // n_mp
+        split = values.reshape(n_z, 2, rows, values.shape[1])
+        keep = lax.dynamic_index_in_dim(split, core, 1, keepdims=False)
+        send = lax.dynamic_index_in_dim(split, 1 - core, 1, keepdims=False).astype(bf16)
+        pair = (keep.astype(f32) + mp_swap(send, 1).astype(f32)).astype(bf16)
+        total = lax.dynamic_index_in_dim(pair, zi, 0, keepdims=False).astype(f32)
+        for step in range(1, n_z):
+            piece = lax.dynamic_index_in_dim(pair, zi ^ step, 0, keepdims=False)
+            total = total + mp_swap(piece, 2 * step).astype(f32)
+        return total
+
+    def gather_rows(values):
+        return lax.all_gather(values, "mp", axis=0, tiled=True)
+
+    ranks = slot_positions(owners, 0)
+    own_slots = owners * capacity + ranks
+    me = di * n_mp + mi
+    hits = own_slots[None, :] == me * capacity + jnp.arange(capacity)[:, None]
+    mine = jnp.sum(jnp.where(hits, jnp.arange(n_blocks)[None, :] + 1, 0), axis=1) - 1
+    count_flat = RANK * (11 * D + 3 * FF) // BLOCK
+    in_order = mine >= count_flat
+    order_matrix = block_order()
+    master_b = master.astype(bf16)
+    ordered = dot(master_b, order_matrix).astype(bf16)
+    to_send = jnp.where(in_order[:, None], master_b, ordered)
+
+    line = jnp.stack([to_send] + [mp_swap(to_send, 2 * step) for step in range(1, n_z)])
+    sheet = plane(line)
+    adapters = jnp.stack([sheet, mp_swap(sheet, 1)])
+    adapters = adapters.reshape(-1, 8, 128)
+    owner_d, owner_m = owners // n_mp, owners % n_mp
+    place = (((owner_m % 2) ^ core) * n_dp + (owner_d ^ di)) * n_z + ((owner_m // 2) ^ zi)
+    place = place * capacity + ranks
+
+    def reshard_line(weights, width):
+        count, rows = weights.shape[0], weights.shape[1]
+        quarter = rows // n_dp
+        part = lax.dynamic_slice_in_dim(weights, di * quarter, quarter, 1)
+        part = part.reshape(count, quarter, n_mp, width).transpose(2, 0, 1, 3)
+        pieces = []
+        for step in range(n_mp):
+            piece = lax.dynamic_index_in_dim(part, mi ^ step, 0, keepdims=False)
+            pieces.append(mp_swap(piece, step) if step else piece)
+        return pieces
+
+    def reshard_plane(pieces):
+        block = jnp.take(jnp.stack(pieces), mi ^ jnp.arange(n_mp), axis=0)
+        whole = plane(block)
+        whole = jnp.take(whole, di ^ jnp.arange(n_dp), axis=0)
+        count, quarter, width = block.shape[1:]
+        whole = whole.reshape(n_dp, n_mp, count, quarter, width).transpose(2, 1, 0, 3, 4)
+        whole = whole.reshape(count, n_mp * n_dp * quarter, width)
+        return [whole[index] for index in range(count)]
+
+    line_a = reshard_line(w_attn[:3], width_a)
+    line_a, w_in_late = lax.optimization_barrier((line_a, w_in))
+    columns_a = reshard_plane(line_a)
+    line_f = reshard_line(w_in_late, width_f)
+    columns_a, line_f = lax.optimization_barrier((columns_a, line_f))
+    columns_f = reshard_plane(line_f)
+    columns = {0: columns_a[0], 1: columns_a[1], 2: columns_a[2], 4: columns_f[0], 5: columns_f[1]}
+    rows_w = {3: w_attn[3], 6: w_down}
+
+    starts = []
+    total_blocks = 0
+    for inner, outer in proj_dims():
+        starts.append(total_blocks)
+        total_blocks += inner * RANK // BLOCK
+    upper_starts = []
+    for inner, outer in proj_dims():
+        upper_starts.append(total_blocks)
+        total_blocks += outer * RANK // BLOCK
+    wanted = []
+    spans = {}
+
+    def want(name, base, count):
+        even = (count + 1) // 2 * 2
+        spans[name] = (sum(w.shape[0] for w in wanted) * 64, count * 64)
+        steps = jnp.minimum(jnp.arange(even), count - 1)
+        wanted.append(base + steps)
+
+    per_a, per_f = width_a * RANK // BLOCK, width_f * RANK // BLOCK
+    for index in (0, 1, 2, 4, 5):
+        per = per_a if index < 3 else per_f
+        want(("A", index), starts[index], D * RANK // BLOCK)
+        want(("B", index), upper_starts[index] + mi * per, per)
+    for index in (3, 6):
+        per = per_a if index == 3 else per_f
+        want(("A", index), starts[index] + mi * per, per)
+        want(("B", index), upper_starts[index], D * RANK // BLOCK)
+    chosen = jnp.take(place, jnp.concatenate(wanted))
+    pairs = jnp.take(adapters, chosen, axis=0).reshape(-1, 2, 8, 128)
+    even, odd = pairs[:, 0], pairs[:, 1]
+    tiles = jnp.concatenate(
+        [
+            jnp.concatenate([even[..., :64], odd[..., :64]], axis=-1),
+            jnp.concatenate([even[..., 64:], odd[..., 64:]], axis=-1),
+        ],
+        axis=1,
+    )
+    flat = tiles.transpose(1, 0, 2).reshape(RANK, -1)
+
+    def adapter(kind, index):
+        start, size = spans[(kind, index)]
+        return flat[:, start : start + size]
+
+    lower = {index: adapter("A", index) for index in range(7)}
+    upper = {index: adapter("B", index) for index in range(7)}
+    magnitude_rows = jnp.take(adapters, place[count_flat:], axis=0).reshape(-1).astype(f32)
+    magnitudes = {}
+    offset = 0
+    for index, (inner, outer) in enumerate(proj_dims()):
+        values = magnitude_rows[offset : offset + outer]
+        if index in columns:
+            width = outer // n_mp
+            values = lax.dynamic_slice_in_dim(values, mi * width, width, 0)
+        magnitudes[index] = values
+        offset += outer
+
+    def squares(weights, index):
+        joined = weights.astype(f32) + dora_scale * dot_first(lower[index], upper[index])
+        return jnp.sum(joined * joined, axis=0)
+
+    norms, scales = {}, {}
+    for index in (0, 1, 2, 4, 5):
+        norms[index] = jnp.sqrt(squares(columns[index], index) + column_eps)
+    both = lax.psum(jnp.stack([squares(rows_w[3], 3), squares(rows_w[6], 6)]), "mp")
+    norms[3] = jnp.sqrt(both[0] + column_eps)
+    norms[6] = jnp.sqrt(both[1] + column_eps)
+    for index in range(7):
+        scales[index] = magnitudes[index] / norms[index]
+
+    def low_rank(inputs, index):
+        return dot_t(inputs, lower[index])
+
+    def project(inputs, weights, index):
+        low = low_rank(inputs, index)
+        return dot(inputs, weights) + dora_scale * wide(low, upper[index]), low
+
+    row = segments[0]
+    positions = segment_positions(row)
+    cosine, sine = rotary_tables(positions)
+    cosine, sine = cosine[:, 0], sine[:, 0]
+    cos_full = jnp.concatenate([cosine, cosine], axis=-1)[:, None, :]
+    sin_full = jnp.concatenate([-sine, sine], axis=-1)[:, None, :]
+    order = jnp.arange(group_rows)
+    allowed = (row[:, None] == row[None, :]) & (order[None, :] <= order[:, None])
+
+    xf = tokens.astype(f32)
+    features = rms_norm(xf, norm_gains[0]).astype(bf16)
+    mixed, lows, heads = {}, {}, {}
+    for index in range(3):
+        mixed[index], lows[index] = project(features, columns[index], index)
+        value = (mixed[index] * scales[index]).reshape(group_rows, n_heads, HEAD_DIM)
+        if index < 2:
+            value = value * cos_full + swap_halves(value) * sin_full
+        heads[index] = value.astype(bf16)
+    query, keys, value = heads[0], heads[1], heads[2]
+    scores = jnp.einsum("thd,shd->hts", query, keys, preferred_element_type=f32) * score_scale
+    scores = jnp.where(allowed[None], scores, -1e30)
+    top = jnp.max(scores, axis=-1, keepdims=True)
+    expd = jnp.exp(scores - top)
+    weights = expd / jnp.sum(expd, axis=-1, keepdims=True)
+    weights_b = weights.astype(bf16)
+    attended = jnp.einsum("hts,shd->thd", weights_b, value, preferred_element_type=f32)
+    attended = attended.reshape(group_rows, width_a).astype(bf16)
+
+    def rows_here(values):
+        return lax.dynamic_slice_in_dim(values, mi * share, share, 0)
+
+    partial, lows[3] = project(attended, rows_w[3], 3)
+    mixed[3] = scatter_rows(partial)
+    x_two = rows_here(tokens).astype(f32) + mixed[3] * scales[3]
+    features_two = gather_rows(rms_norm(x_two, norm_gains[1]).astype(bf16))
+    for index in (4, 5):
+        mixed[index], lows[index] = project(features_two, columns[index], index)
+    gate = mixed[4] * scales[4]
+    upward = mixed[5] * scales[5]
+    sigmoid_gate = jax.nn.sigmoid(gate)
+    act = (gate * sigmoid_gate * upward).astype(bf16)
+    partial, lows[6] = project(act, rows_w[6], 6)
+    mixed[6] = scatter_rows(partial)
+    layer_out = gather_rows((x_two + mixed[6] * scales[6]).astype(bf16))
+
+    def send_back(grad, index):
+        grad_b = (grad * scales[index]).astype(bf16)
+        through = dora_scale * dot_t(grad_b, upper[index])
+        return grad_b, through
+
+    def to_inputs(grad_b, through, weights, index):
+        return dot_t(grad_b, weights) + wide(through, lower[index])
+
+    def dots_of(grad, index):
+        return jnp.sum(grad * mixed[index], axis=0)
+
+    grad_out = cotangent.astype(f32)
+    grads_b, throughs, dots = {}, {}, {}
+    grads_b[6], throughs[6] = send_back(grad_out, 6)
+    grad_act = to_inputs(grads_b[6], throughs[6], rows_w[6], 6)
+    grad_gate = grad_act * upward * sigmoid_gate * (1.0 + gate * (1.0 - sigmoid_gate))
+    grad_up = grad_act * gate * sigmoid_gate
+    back = 0.0
+    for index, grad in ((4, grad_gate), (5, grad_up)):
+        dots[index] = dots_of(grad, index)
+        grads_b[index], throughs[index] = send_back(grad, index)
+        back = back + to_inputs(grads_b[index], throughs[index], columns[index], index)
+    out_here = rows_here(cotangent).astype(f32)
+    grad_two = out_here + rms_back(x_two, scatter_rows(back), norm_gains[1])
+    grads_b[3] = gather_rows((grad_two * scales[3]).astype(bf16))
+    throughs[3] = dora_scale * dot_t(grads_b[3], upper[3])
+    grad_att = to_inputs(grads_b[3], throughs[3], rows_w[3], 3).astype(bf16)
+    grad_att = grad_att.reshape(group_rows, n_heads, HEAD_DIM)
+    grad_weights = jnp.einsum("thd,shd->hts", grad_att, value, preferred_element_type=f32)
+    grad_value = jnp.einsum("hts,thd->shd", weights_b, grad_att, preferred_element_type=f32)
+    centred = jnp.sum(weights * grad_weights, axis=-1, keepdims=True)
+    grad_scores = (weights * (grad_weights - centred)).astype(bf16)
+    grad_query = jnp.einsum("hts,shd->thd", grad_scores, keys, preferred_element_type=f32)
+    grad_key = jnp.einsum("hts,thd->shd", grad_scores, query, preferred_element_type=f32)
+    incoming = []
+    for grad in (grad_query, grad_key):
+        grad = grad * score_scale
+        incoming.append((grad * cos_full - swap_halves(grad) * sin_full).reshape(group_rows, width_a))
+    incoming.append(grad_value.reshape(group_rows, width_a))
+    back = 0.0
+    for index, grad in enumerate(incoming):
+        dots[index] = dots_of(grad, index)
+        grads_b[index], throughs[index] = send_back(grad, index)
+        back = back + to_inputs(grads_b[index], throughs[index], columns[index], index)
+    grad_in = grad_two + rms_back(rows_here(tokens).astype(f32), scatter_rows(back), norm_gains[0])
+    input_grad = gather_rows(grad_in.astype(bf16)).astype(f32)
+
+    here = jnp.stack([dots_of(grad_two, 3), dots_of(out_here, 6)])
+    both = lax.psum(here, "mp")
+    dots[3], dots[6] = both[0], both[1]
+    inputs = {0: features, 1: features, 2: features, 3: attended, 4: features_two, 5: features_two, 6: act}
+    grad_lower, grad_upper = {}, {}
+    for index in range(7):
+        weights_p = columns[index] if index in columns else rows_w[index]
+        norm = norms[index]
+        ratio = -dots[index] * magnitudes[index] / (norm * norm * norm)
+        upper_f = upper[index].astype(f32)
+        scaled = dora_scale * upper_f * ratio[None, :]
+        grad_lower[index] = (
+            wide_first(throughs[index], inputs[index])
+            + wide_t(scaled, weights_p)
+            + wide(dora_scale * wide_t(scaled, upper_f), lower[index])
+        )
+        crossed = dot(lower[index], weights_p) + dora_scale * wide(
+            dot_t(lower[index], lower[index]), upper[index]
+        )
+        grad_upper[index] = dora_scale * (
+            wide_first(lows[index], grads_b[index]) + crossed * ratio[None, :]
+        )
+    grad_magnitude = []
+    for index, (inner, outer) in enumerate(proj_dims()):
+        if index in columns:
+            width = outer // n_mp
+            full = jnp.zeros((outer,), f32)
+            full = lax.dynamic_update_slice_in_dim(full, dots[index] / norms[index], mi * width, 0)
+        else:
+            full = here[0 if index == 3 else 1] / norms[index]
+        grad_magnitude.append(full)
+
+    def to_blocks(values):
+        extra = -values.shape[1] % 128
+        if extra:
+            values = jnp.pad(values, ((0, 0), (0, extra)))
+        parts = values.reshape(2, 8, -1, 128).transpose(2, 0, 1, 3)
+        low, high = parts[:, 0], parts[:, 1]
+        even = jnp.concatenate([low[..., :64], high[..., :64]], axis=-1)
+        odd = jnp.concatenate([low[..., 64:], high[..., 64:]], axis=-1)
+        return jnp.stack([even, odd], axis=1).reshape(-1, BLOCK)
+
+    shared = []
+    where = {}
+    shared_rows = 0
+
+    def add_shared(name, blocks):
+        nonlocal shared_rows
+        where[name] = ("shared", shared_rows)
+        shared.append(blocks)
+        shared_rows += blocks.shape[0]
+
+    for index in (0, 1, 2, 4, 5):
+        add_shared(("A", index), to_blocks(grad_lower[index]))
+    for index in (3, 6):
+        add_shared(("B", index), to_blocks(grad_upper[index]))
+    add_shared("m", jnp.concatenate(grad_magnitude).reshape(-1, BLOCK))
+    unit = -(-shared_rows // n_mp)
+    shared.append(jnp.zeros((unit * n_mp - shared_rows, BLOCK), f32))
+    summed = scatter_rows(jnp.concatenate(shared))
+    local = [summed]
+    local_rows = unit
+
+    for index in (3, 6):
+        blocks = to_blocks(grad_lower[index])
+        where[("A", index)] = ("local", local_rows)
+        local.append(blocks)
+        local_rows += blocks.shape[0]
+    for index in (0, 1, 2, 4, 5):
+        blocks = to_blocks(grad_upper[index])
+        where[("B", index)] = ("local", local_rows)
+        local.append(blocks)
+        local_rows += blocks.shape[0]
+    part = -(-local_rows // n_dp)
+    local.append(jnp.zeros((part * n_dp - local_rows, BLOCK), f32))
+    local = jnp.concatenate(local).reshape(n_dp, part, BLOCK).astype(bf16)
+    total = lax.dynamic_index_in_dim(local, di, 0, keepdims=False).astype(f32)
+    for step in range(1, n_dp):
+        piece = lax.dynamic_index_in_dim(local, di ^ step, 0, keepdims=False)
+        total = total + dp_swap(piece, step).astype(f32)
+    reduced = lax.all_gather(total.astype(bf16), ("dp", "mp"), axis=0, tiled=True)
+
+    table = np.zeros((n_blocks,), np.int32)
+
+    def set_row(block, m, local_row):
+        table[block] = ((local_row // part) * n_mp + m) * part + local_row % part
+
+    for index, (inner, outer) in enumerate(proj_dims()):
+        for kind, base, size in (("A", starts[index], inner), ("B", upper_starts[index], outer)):
+            count = size * RANK // BLOCK
+            space, begin = where[(kind, index)]
+            for k in range(count):
+                if space == "shared":
+                    set_row(base + k, (begin + k) // unit, (begin + k) % unit)
+                else:
+                    per = count // n_mp
+                    set_row(base + k, k // per, begin + k % per)
+    begin = where["m"][1]
+    for k in range(n_blocks - count_flat):
+        set_row(count_flat + k, (begin + k) // unit, (begin + k) % unit)
+    picked = jnp.take(reduced, jnp.take(jnp.asarray(table), jnp.maximum(mine, 0)), axis=0)
+    unordered = dot_t(picked, order_matrix)
+    grad = jnp.where(in_order[:, None], picked.astype(f32), unordered)
+    grad = jnp.where((mine >= 0)[:, None], grad, 0.0)
+    new_master, new_first, new_second = adam_update(
+        master, grad, first_moment, second_moment, block_rates(mine)
+    )
+    return (layer_out, input_grad, new_master, new_first, new_second)
+
+
 def solution(mesh):
+    fast = mesh.shape["dp"] == 4 and mesh.shape["mp"] == 8
     return jax.shard_map(
-        body,
+        fast_body if fast else body,
         mesh=mesh,
         in_specs=(
             P("dp", None),

time: 1580 us -> 660 us (0.42)
  waiting for transfers between devices: 1000 us -> 154 us
  other arithmetic: 167 us -> 75.6 us
  matrix products: 218 us -> 137 us
  starting transfers between devices: 0.88 us -> 76.2 us
  blocking collectives: 0 us -> 66.4 us
  local copies, waits for them, and re-layouts: 148 us -> 122 us
    psum x6 -> x0, waiting for transfers between devices: 716 us -> none  [the longest x3 425 us: finish(): summed_mixed, summed_low = lax.psum((local_mixed, local_low), 'mp')]
    reduce_scatter x1 -> x0, waiting for transfers between devices: 129 us -> none  [body(): lax.psum_scatter(buffer, ('dp', 'mp'), scatter_dimension=0, tiled=True)]
    all_gather x5, waiting for transfers between devices: 158 us -> 56.5 us  [the longest x1 35 us: fast_body(): lax.all_gather(total.astype(bf16), ('dp', 'mp'), axis=0, tiled=True)]
    ppermute x0 -> x59, waiting for transfers between devices: none -> 97.2 us  [the longest x38 76.8 us: mp_swap(): return lax.ppermute(values, 'mp', [(i, i ^ step) for i in range(n_mp)])]
    dot_general x83 -> x112, matrix products: 218 us -> 134 us  [the longest x43 55.8 us: dot_t(): lax.dot_general(left, right, (((1,), (1,)), ((), ())), preferred_element_...]
    ppermute x0 -> x59, starting transfers between devices: none -> 75.6 us  [the longest x38 57.7 us: mp_swap(): return lax.ppermute(values, 'mp', [(i, i ^ step) for i in range(n_mp)])]
    psum x0 -> x2, blocking collectives: none -> 66.4 us  [the longest x1 42.2 us: fast_body(): lax.psum(jnp.stack([squares(rows_w[3], 3), squares(rows_w[6], 6)]), 'mp')]
    reshape x33 -> x3, local copies, waits for them, and re-layouts: 54.1 us -> 5.63 us  [the longest x1 3 us: reshard_line(): part = part.reshape(count, quarter, n_mp, width).transpose(2, 0, 1, 3)]
  transfers between devices with their start and end apart: 12 -> 64, of which waited for: 10 -> 19; matrix products, arithmetic and copies ran while one was open for 14% -> 43% of each run, Pallas kernels for 0% -> 0%
where the time goes in v1:
time: 660 us; the launch traced here: 649 us
  waiting for transfers between devices  154 us (23%)
  matrix products  137 us (21%)
  local copies, waits for them, and re-layouts  122 us (18%)
  starting transfers between devices  76.2 us (12%)
  other arithmetic  75.6 us (11%)
  blocking collectives  66.4 us (10%)
  between operations  17.6 us (3%)
    ppermute x38, waiting for transfers between devices, mp_swap(): return lax.ppermute(values, 'mp', [(i, i ^ step) for i in range(n_mp)])  76.8 us
    ppermute x38, starting transfers between devices, mp_swap(): return lax.ppermute(values, 'mp', [(i, i ^ step) for i in range(n_mp)])  57.7 us
    dot_general x43, matrix products, dot_t(): lax.dot_general(left, right, (((1,), (1,)), ((), ())), preferred_element_...  55.8 us
    dot_general x43, matrix products, dot(): return jnp.dot(left, right, preferred_element_type=jnp.float32, **kwargs)  50.1 us
    psum x1, blocking collectives, fast_body(): lax.psum(jnp.stack([squares(rows_w[3], 3), squares(rows_w[6], 6)]), 'mp')  42.2 us
    unnamed x427, local copies, waits for them, and re-layouts  35.6 us
    all_gather x1, waiting for transfers between devices, fast_body(): lax.all_gather(total.astype(bf16), ('dp', 'mp'), axis=0, tiled=True)  35 us
    psum x1, blocking collectives, fast_body(): both = lax.psum(here, 'mp')  24.2 us
  transfers between devices with their start and end apart: 64, of which 19 were waited for; matrix products, arithmetic and copies ran while one was open for 43% of the time, Pallas kernels for 0%

profile of v1, /device:TPU:1, one launch (start us, length us, event | category | flops | bytes accessed | tf_op | source)
XLA Modules:
  0.0 648.7 jit_solution(5874682190052853170)
XLA Ops:
  11.4 2.7 fusion.37
  14.2 4.2 collective-permute-start.25
  18.8 4.0 slice.481
  44.6 3.5 collective-permute-start.5
  52.3 5.9 collective-permute-done.4
  65.7 3.0 reshape.1090
  71.5 3.6 constant_dynamic-slice_fusion
  89.6 3.1 collective-permute-start.14
  92.7 5.3 collective-permute-done.12
  98.1 5.3 collective-permute-start.15
  104.7 2.8 collective-permute-start.17
  110.7 4.4 gather_fusion.1
  118.8 2.8 collective-permute-start.19
  123.6 9.1 %collective-permute-done.17 = bf16[2,64,704]{2,1,0:T(8,128)(2,1)S(1)} collective-permute-done((bf16[2,64,704]{2,1,0:T(8,128)(2,1)}, bf16[2,64,704]{2,1,0:T(8,128)(2,1)S(1)}, u32[]{:S(2)}, u32[]{:S(2)}) %collective-permute-start.17) | collective-permute-done | bytes 180256 | tf_op jit(solution)/shard_map/ppermute | solution.py:440
  146.9 14.5 %collective-permute-done.38 = bf16[4,2,64,704]{3,2,1,0:T(8,128)(2,1)} collective-permute-done((bf16[4,2,64,704]{3,2,1,0:T(8,128)(2,1)}, bf16[4,2,64,704]{3,2,1,0:T(8,128)(2,1)}, u32[]{:S(2)}, u32[]{:S(2)}) %collective-permute-start.38) | collective-permute-done | bytes 720928 | tf_op jit(solution)/shard_map/ppermute | solution.py:443
  178.2 3.1 gather_fusion.4
  184.1 42.2 %psum.14 = f32[2,2048]{1,0:T(2,128)S(1)} all-reduce(f32[2,2048]{1,0:T(2,128)S(1)} %pad_maximum_fusion.18), channel_id=1, replica_groups=mesh['dp'=4,'mp'=8] {'mp'}, use_global_device_ids=true, to_apply=%region_12.13 | all-reduce | flops 4096 | bytes 32768 | tf_op jit(solution)/shard_map/psum | solution.py:580
  229.7 4.5 fusion.26
  247.8 2.7 fusion.371
  258.6 4.2 collective-permute-start.30
  274.3 3.2 pad_maximum_fusion
  277.5 6.5 %gather_fusion.6 = bf16[4,2,4,2,64,704]{5,4,3,2,1,0:T(8,128)(2,1)} fusion(bf16[4,2,4,2,64,704]{5,4,3,2,1,0:T(8,128)(2,1)} %pad_maximum_fusion, s32[1024]{0:T(1024)} %get-tuple-element.292), kind=kCustom, calls=%fused_computation.6 | custom fusion | bytes 11534352 | tf_op jit(solution)/shard_map/jit(_take)/gather | solution.py:502
  284.1 7.2 %collective-permute-done.32 = bf16[48,2048]{1,0:T(8,128)(2,1)} collective-permute-done((bf16[48,2048]{1,0:T(8,128)(2,1)}, bf16[48,2048]{1,0:T(8,128)(2,1)}, u32[]{:S(2)}, u32[]{:S(2)}) %collective-permute-start.32) | collective-permute-done | bytes 196640 | tf_op jit(solution)/shard_map/ppermute | solution.py:440
  294.4 3.5 fusion.1
  297.9 3.1 fusion.333
  301.0 4.7 copy.147
  305.7 5.1 copy.146
  310.8 3.2 multiply_reduce_fusion
  323.2 3.6 fusion.373
  362.7 3.0 collective-permute-done.43
  365.8 17.9 %collective-permute-done.42 = bf16[48,2048]{1,0:T(8,128)(2,1)S(1)} collective-permute-done((bf16[48,2048]{1,0:T(8,128)(2,1)S(1)}, bf16[48,2048]{1,0:T(8,128)(2,1)S(1)}, u32[]{:S(2)}, u32[]{:S(2)}) %collective-permute-start.42) | collective-permute-done | bytes 196640 | tf_op jit(solution)/shard_map/ppermute | solution.py:440
  383.7 8.4 %collective-permute-done.46 = bf16[48,2048]{1,0:T(8,128)(2,1)S(1)} collective-permute-done((bf16[48,2048]{1,0:T(8,128)(2,1)S(1)}, bf16[48,2048]{1,0:T(8,128)(2,1)S(1)}, u32[]{:S(2)}, u32[]{:S(2)}) %collective-permute-start.46) | collective-permute-done | bytes 196640 | tf_op jit(solution)/shard_map/ppermute | solution.py:440
  400.7 4.4 convolution_add_fusion.3
  408.2 24.2 %psum.15 = f32[2,2048]{1,0:T(2,128)} all-reduce(f32[2,2048]{1,0:T(2,128)} %pad_maximum_fusion.19), channel_id=1, replica_groups=mesh['dp'=4,'mp'=8] {'mp'}, use_global_device_ids=true, to_apply=%region_27.28 | all-reduce | flops 4096 | bytes 32768 | tf_op jit(solution)/shard_map/psum | solution.py:686
  440.2 2.7 fusion.108
  455.3 3.2 fusion.164
  459.9 3.2 fusion.173
  463.7 3.1 fusion.182
  509.9 6.4 concatenate.253
  518.7 4.8 collective-permute-start.52
  526.2 6.9 %add_add_fusion = f32[384,2048]{1,0:T(8,128)} fusion(f32[384,2048]{1,0:T(8,128)} %fusion.182, f32[384,2048]{1,0:T(8,128)S(1)} %fusion.378, f32[384,2048]{1,0:T(8,128)S(1)} %copy-done.14, f32[384,2048]{1,0:T(8,128)} %fusion.377, f32[384,2048]{1,0:T(8,128)} %fusion.173, bf16[384,256]{0,1:T(8,128)(2,1)S(1)} %get-tuple-element.124, ...), kind=kOutput, calls=%fused_computation.27 | convolution fusion | flops 406585344 | bytes 20119552 | tf_op jit(solution)/shard_map/dot_general | solution.py:375
  539.1 2.9 collective-permute-done.54
  555.9 3.1 collective-permute-done.49
  559.0 3.8 collective-permute-done.51
  562.8 10.3 %collective-permute-done.50 = bf16[48,2048]{1,0:T(8,128)(2,1)S(1)} collective-permute-done((bf16[48,2048]{1,0:T(8,128)(2,1)S(1)}, bf16[48,2048]{1,0:T(8,128)(2,1)S(1)}, u32[]{:S(2)}, u32[]{:S(2)}) %collective-permute-start.50) | collective-permute-done | bytes 196640 | tf_op jit(solution)/shard_map/ppermute | solution.py:440
  576.3 35.0 %all-gather.15.cloned.1.call-done = bf16[32,21,1024]{2,1,0:T(8,128)(2,1)} async-done(((bf16[1,21,1024]{2,1,0:T(8,128)(2,1)}), bf16[32,21,1024]{2,1,0:T(8,128)(2,1)}) %all-gather.15.cloned.1.call-update) | async-done | bytes 1376272 | tf_op jit(solution)/shard_map/all_gather | solution.py:765
  615.9 21.5 %all-gather.13.cloned.1.call-done = bf16[384,2048]{1,0:T(8,128)(2,1)} async-done(((bf16[48,2048]{1,0:T(8,128)(2,1)}), bf16[384,2048]{1,0:T(8,128)(2,1)}) %all-gather.13.cloned.1.call-update) | async-done | bytes 1572880 | tf_op jit(solution)/shard_map/all_gather | solution.py:466
  637.3 3.4 convert_element_type.449
  (901 shorter events, 291.7 us)
Async XLA Ops:
  7.2 314.0 %all-gather.7.cloned.1.call-start = ((), (), s32[]{:S(2)}) async-start(), calls=%async_computation | async-start | bytes 1769472 | tf_op jit(solution)/shard_map/all_gather | solution.py:466
  14.2 27.7 %collective-permute-start.25 = (bf16[40,1024]{1,0:T(8,128)(2,1)}, bf16[40,1024]{1,0:T(8,128)(2,1)S(1)}, u32[]{:S(2)}, u32[]{:S(2)}) collective-permute-start(bf16[40,1024]{1,0:T(8,128)(2,1)} %fusion.37), channel_id=1, source_target_pairs={{0,6},{1,7},{2,4},{3,5},{4,2},{5,3},{6,0},{7,1},{8,14},{9,15},{10,... | collective-permute-start | bytes 245768 | tf_op jit(solution)/shard_map/ppermute | solution.py:440
  18.5 25.6 %collective-permute-start.24 = (bf16[40,1024]{1,0:T(8,128)(2,1)}, bf16[40,1024]{1,0:T(8,128)(2,1)}, u32[]{:S(2)}, u32[]{:S(2)}) collective-permute-start(bf16[40,1024]{1,0:T(8,128)(2,1)} %fusion.37), channel_id=1, source_target_pairs={{0,4},{1,5},{2,6},{3,7},{4,0},{5,1},{6,2},{7,3},{8,12},{9,13},{10,... | collective-permute-start | bytes 245768 | tf_op jit(solution)/shard_map/ppermute | solution.py:440
  18.5 21.2 %collective-permute-start.20 = (bf16[40,1024]{1,0:T(8,128)(2,1)}, bf16[40,1024]{1,0:T(8,128)(2,1)}, u32[]{:S(2)}, u32[]{:S(2)}) collective-permute-start(bf16[40,1024]{1,0:T(8,128)(2,1)} %fusion.37), channel_id=1, source_target_pairs={{0,2},{1,3},{2,0},{3,1},{4,6},{5,7},{6,4},{7,5},{8,10},{9,11},{10,... | collective-permute-start | bytes 245768 | tf_op jit(solution)/shard_map/ppermute | solution.py:440
  26.8 17.8 %collective-permute-start = (bf16[3,64,256]{2,1,0:T(8,128)(2,1)S(1)}, bf16[3,64,256]{2,1,0:T(8,128)(2,1)S(1)}, u32[]{:S(2)}, u32[]{:S(2)}) collective-permute-start(bf16[3,64,256]{2,1,0:T(8,128)(2,1)S(1)} %bitcast.966), channel_id=1, source_target_pairs={{0,1},{1,0},{2,3},{3,2},{4,5},{5,4},{6,7},{7,6},{8,9},{9,8},{10,11... | collective-permute-start | bytes 294920 | tf_op jit(solution)/shard_map/ppermute | solution.py:440
  28.1 20.0 %collective-permute-start.1 = (bf16[3,64,256]{2,1,0:T(8,128)(2,1)S(1)}, bf16[3,64,256]{2,1,0:T(8,128)(2,1)S(1)}, u32[]{:S(2)}, u32[]{:S(2)}) collective-permute-start(bf16[3,64,256]{2,1,0:T(8,128)(2,1)S(1)} %bitcast.965), channel_id=1, source_target_pairs={{0,2},{1,3},{2,0},{3,1},{4,6},{5,7},{6,4},{7,5},{8,10},{9,11},{10,... | collective-permute-start | bytes 294920 | tf_op jit(solution)/shard_map/ppermute | solution.py:440
  44.0 14.2 %collective-permute-start.4 = (bf16[3,64,256]{2,1,0:T(8,128)(2,1)S(1)}, bf16[3,64,256]{2,1,0:T(8,128)(2,1)S(1)}, u32[]{:S(2)}, u32[]{:S(2)}) collective-permute-start(bf16[3,64,256]{2,1,0:T(8,128)(2,1)S(1)} %bitcast.969), channel_id=1, source_target_pairs={{0,5},{1,4},{2,7},{3,6},{4,1},{5,0},{6,3},{7,2},{8,13},{9,12},{10,... | collective-permute-start | bytes 294920 | tf_op jit(solution)/shard_map/ppermute | solution.py:440
  44.6 15.1 %collective-permute-start.5 = (bf16[3,64,256]{2,1,0:T(8,128)(2,1)S(1)}, bf16[3,64,256]{2,1,0:T(8,128)(2,1)S(1)}, u32[]{:S(2)}, u32[]{:S(2)}) collective-permute-start(bf16[3,64,256]{2,1,0:T(8,128)(2,1)S(1)} %bitcast.968), channel_id=1, source_target_pairs={{0,6},{1,7},{2,4},{3,5},{4,2},{5,3},{6,0},{7,1},{8,14},{9,15},{10,... | collective-permute-start | bytes 294920 | tf_op jit(solution)/shard_map/ppermute | solution.py:440
  48.1 11.6 %collective-permute-start.6 = (bf16[3,64,256]{2,1,0:T(8,128)(2,1)S(1)}, bf16[3,64,256]{2,1,0:T(8,128)(2,1)S(1)}, u32[]{:S(2)}, u32[]{:S(2)}) collective-permute-start(bf16[3,64,256]{2,1,0:T(8,128)(2,1)S(1)} %bitcast.967), channel_id=1, source_target_pairs={{0,7},{1,6},{2,5},{3,4},{4,3},{5,2},{6,1},{7,0},{8,15},{9,14},{10,... | collective-permute-start | bytes 294920 | tf_op jit(solution)/shard_map/ppermute | solution.py:440
  49.9 18.9 %collective-permute-start.26 = (bf16[2,40,1024]{2,1,0:T(8,128)(2,1)}, bf16[2,40,1024]{2,1,0:T(8,128)(2,1)}, u32[]{:S(2)}, u32[]{:S(2)}) collective-permute-start(bf16[2,40,1024]{2,1,0:T(8,128)(2,1)} %get-tuple-element.156), channel_id=1, source_target_pairs={{0,8},{8,0},{16,24},{24,16},{1,9},{9,1},{17,25},{25,17},{2,10},{10... | collective-permute-start | bytes 491528 | tf_op jit(solution)/shard_map/ppermute | solution.py:443
  51.1 17.7 %collective-permute-start.27 = (bf16[2,40,1024]{2,1,0:T(8,128)(2,1)}, bf16[2,40,1024]{2,1,0:T(8,128)(2,1)}, u32[]{:S(2)}, u32[]{:S(2)}) collective-permute-start(bf16[2,40,1024]{2,1,0:T(8,128)(2,1)} %get-tuple-element.156), channel_id=1, source_target_pairs={{0,16},{8,24},{16,0},{24,8},{1,17},{9,25},{17,1},{25,9},{2,18},{10... | collective-permute-start | bytes 491528 | tf_op jit(solution)/shard_map/ppermute | solution.py:443
  58.2 12.0 %collective-permute-start.21 = (bf16[2,40,1024]{2,1,0:T(8,128)(2,1)}, bf16[2,40,1024]{2,1,0:T(8,128)(2,1)}, u32[]{:S(2)}, u32[]{:S(2)}) collective-permute-start(bf16[2,40,1024]{2,1,0:T(8,128)(2,1)} %get-tuple-element.154), channel_id=1, source_target_pairs={{0,8},{8,0},{16,24},{24,16},{1,9},{9,1},{17,25},{25,17},{2,10},{10... | collective-permute-start | bytes 491528 | tf_op jit(solution)/shard_map/ppermute | solution.py:443
  61.7 18.8 %collective-permute-start.11 = (bf16[4,3,64,256]{3,2,1,0:T(8,128)(2,1)}, bf16[4,3,64,256]{3,2,1,0:T(8,128)(2,1)}, u32[]{:S(2)}, u32[]{:S(2)}) collective-permute-start(bf16[4,3,64,256]{3,2,1,0:T(8,128)(2,1)} %get-tuple-element.111), channel_id=1, source_target_pairs={{0,16},{8,24},{16,0},{24,8},{1,17},{9,25},{17,1},{25,9},{2,18},{10... | collective-permute-start | bytes 1179656 | tf_op jit(solution)/shard_map/ppermute | solution.py:443
  62.9 22.8 %collective-permute-start.7 = (bf16[4,3,64,256]{3,2,1,0:T(8,128)(2,1)}, bf16[4,3,64,256]{3,2,1,0:T(8,128)(2,1)}, u32[]{:S(2)}, u32[]{:S(2)}) collective-permute-start(bf16[4,3,64,256]{3,2,1,0:T(8,128)(2,1)} %get-tuple-element.112), channel_id=1, source_target_pairs={{0,8},{8,0},{16,24},{24,16},{1,9},{9,1},{17,25},{25,17},{2,10},{10... | collective-permute-start | bytes 1179656 | tf_op jit(solution)/shard_map/ppermute | solution.py:443
  68.7 14.0 %collective-permute-start.22 = (bf16[2,40,1024]{2,1,0:T(8,128)(2,1)}, bf16[2,40,1024]{2,1,0:T(8,128)(2,1)S(1)}, u32[]{:S(2)}, u32[]{:S(2)}) collective-permute-start(bf16[2,40,1024]{2,1,0:T(8,128)(2,1)} %get-tuple-element.154), channel_id=1, source_target_pairs={{0,16},{8,24},{16,0},{24,8},{1,17},{9,25},{17,1},{25,9},{2,18},{10... | collective-permute-start | bytes 491528 | tf_op jit(solution)/shard_map/ppermute | solution.py:443
  68.8 11.3 %collective-permute-start.28 = (bf16[2,40,1024]{2,1,0:T(8,128)(2,1)}, bf16[2,40,1024]{2,1,0:T(8,128)(2,1)S(1)}, u32[]{:S(2)}, u32[]{:S(2)}) collective-permute-start(bf16[2,40,1024]{2,1,0:T(8,128)(2,1)} %collective-permute-done.27), channel_id=1, source_target_pairs={{0,8},{8,0},{16,24},{24,16},{1,9},{9,1},{17,25},{25,17},{2,10},{10... | collective-permute-start | bytes 491528 | tf_op jit(solution)/shard_map/ppermute | solution.py:443
  70.2 12.8 %collective-permute-start.23 = (bf16[2,40,1024]{2,1,0:T(8,128)(2,1)}, bf16[2,40,1024]{2,1,0:T(8,128)(2,1)S(1)}, u32[]{:S(2)}, u32[]{:S(2)}) collective-permute-start(bf16[2,40,1024]{2,1,0:T(8,128)(2,1)} %collective-permute-done.21), channel_id=1, source_target_pairs={{0,16},{8,24},{16,0},{24,8},{1,17},{9,25},{17,1},{25,9},{2,18},{10... | collective-permute-start | bytes 491528 | tf_op jit(solution)/shard_map/ppermute | solution.py:443
  80.4 17.6 %collective-permute-start.12 = (bf16[4,3,64,256]{3,2,1,0:T(8,128)(2,1)}, bf16[4,3,64,256]{3,2,1,0:T(8,128)(2,1)S(1)}, u32[]{:S(2)}, u32[]{:S(2)}) collective-permute-start(bf16[4,3,64,256]{3,2,1,0:T(8,128)(2,1)} %collective-permute-done.11), channel_id=1, source_target_pairs={{0,8},{8,0},{16,24},{24,16},{1,9},{9,1},{17,25},{25,17},{2,10},{10... | collective-permute-start | bytes 1179656 | tf_op jit(solution)/shard_map/ppermute | solution.py:443
  82.7 21.9 %collective-permute-start.8 = (bf16[4,3,64,256]{3,2,1,0:T(8,128)(2,1)}, bf16[4,3,64,256]{3,2,1,0:T(8,128)(2,1)S(1)}, u32[]{:S(2)}, u32[]{:S(2)}) collective-permute-start(bf16[4,3,64,256]{3,2,1,0:T(8,128)(2,1)} %get-tuple-element.112), channel_id=1, source_target_pairs={{0,16},{8,24},{16,0},{24,8},{1,17},{9,25},{17,1},{25,9},{2,18},{10... | collective-permute-start | bytes 1179656 | tf_op jit(solution)/shard_map/ppermute | solution.py:443
  83.0 34.4 %collective-permute-start.13 = (bf16[2,64,704]{2,1,0:T(8,128)(2,1)}, bf16[2,64,704]{2,1,0:T(8,128)(2,1)S(1)}, u32[]{:S(2)}, u32[]{:S(2)}) collective-permute-start(bf16[2,64,704]{2,1,0:T(8,128)(2,1)} %bitcast.771), channel_id=1, source_target_pairs={{0,1},{1,0},{2,3},{3,2},{4,5},{5,4},{6,7},{7,6},{8,9},{9,8},{10,11... | collective-permute-start | bytes 540680 | tf_op jit(solution)/shard_map/ppermute | solution.py:440
  85.7 19.0 %collective-permute-start.9 = (bf16[4,3,64,256]{3,2,1,0:T(8,128)(2,1)}, bf16[4,3,64,256]{3,2,1,0:T(8,128)(2,1)S(1)}, u32[]{:S(2)}, u32[]{:S(2)}) collective-permute-start(bf16[4,3,64,256]{3,2,1,0:T(8,128)(2,1)} %collective-permute-done.7), channel_id=1, source_target_pairs={{0,16},{8,24},{16,0},{24,8},{1,17},{9,25},{17,1},{25,9},{2,18},{10... | collective-permute-start | bytes 1179656 | tf_op jit(solution)/shard_map/ppermute | solution.py:443
  89.6 28.5 %collective-permute-start.14 = (bf16[2,64,704]{2,1,0:T(8,128)(2,1)}, bf16[2,64,704]{2,1,0:T(8,128)(2,1)S(1)}, u32[]{:S(2)}, u32[]{:S(2)}) collective-permute-start(bf16[2,64,704]{2,1,0:T(8,128)(2,1)} %bitcast.770), channel_id=1, source_target_pairs={{0,2},{1,3},{2,0},{3,1},{4,6},{5,7},{6,4},{7,5},{8,10},{9,11},{10,... | collective-permute-start | bytes 540680 | tf_op jit(solution)/shard_map/ppermute | solution.py:440
  98.1 25.2 %collective-permute-start.15 = (bf16[2,64,704]{2,1,0:T(8,128)(2,1)}, bf16[2,64,704]{2,1,0:T(8,128)(2,1)}, u32[]{:S(2)}, u32[]{:S(2)}) collective-permute-start(bf16[2,64,704]{2,1,0:T(8,128)(2,1)} %bitcast.769), channel_id=1, source_target_pairs={{0,3},{1,2},{2,1},{3,0},{4,7},{5,6},{6,5},{7,4},{8,11},{9,10},{10,... | collective-permute-start | bytes 540680 | tf_op jit(solution)/shard_map/ppermute | solution.py:440
  104.6 19.0 %collective-permute-start.16 = (bf16[2,64,704]{2,1,0:T(8,128)(2,1)}, bf16[2,64,704]{2,1,0:T(8,128)(2,1)S(1)}, u32[]{:S(2)}, u32[]{:S(2)}) collective-permute-start(bf16[2,64,704]{2,1,0:T(8,128)(2,1)} %bitcast.768), channel_id=1, source_target_pairs={{0,4},{1,5},{2,6},{3,7},{4,0},{5,1},{6,2},{7,3},{8,12},{9,13},{10,... | collective-permute-start | bytes 540680 | tf_op jit(solution)/shard_map/ppermute | solution.py:440
  104.7 28.0 %collective-permute-start.17 = (bf16[2,64,704]{2,1,0:T(8,128)(2,1)}, bf16[2,64,704]{2,1,0:T(8,128)(2,1)S(1)}, u32[]{:S(2)}, u32[]{:S(2)}) collective-permute-start(bf16[2,64,704]{2,1,0:T(8,128)(2,1)} %bitcast.767), channel_id=1, source_target_pairs={{0,5},{1,4},{2,7},{3,6},{4,1},{5,0},{6,3},{7,2},{8,13},{9,12},{10,... | collective-permute-start | bytes 540680 | tf_op jit(solution)/shard_map/ppermute | solution.py:440
  117.5 15.3 %collective-permute-start.18 = (bf16[2,64,704]{2,1,0:T(8,128)(2,1)S(1)}, bf16[2,64,704]{2,1,0:T(8,128)(2,1)S(1)}, u32[]{:S(2)}, u32[]{:S(2)}) collective-permute-start(bf16[2,64,704]{2,1,0:T(8,128)(2,1)S(1)} %bitcast.941), channel_id=1, source_target_pairs={{0,6},{1,7},{2,4},{3,5},{4,2},{5,3},{6,0},{7,1},{8,14},{9,15},{10,... | collective-permute-start | bytes 540680 | tf_op jit(solution)/shard_map/ppermute | solution.py:440
  118.8 14.0 %collective-permute-start.19 = (bf16[2,64,704]{2,1,0:T(8,128)(2,1)S(1)}, bf16[2,64,704]{2,1,0:T(8,128)(2,1)S(1)}, u32[]{:S(2)}, u32[]{:S(2)}) collective-permute-start(bf16[2,64,704]{2,1,0:T(8,128)(2,1)S(1)} %bitcast.940), channel_id=1, source_target_pairs={{0,7},{1,6},{2,5},{3,4},{4,3},{5,2},{6,1},{7,0},{8,15},{9,14},{10,... | collective-permute-start | bytes 540680 | tf_op jit(solution)/shard_map/ppermute | solution.py:440
  123.3 39.6 %collective-permute-start.29 = (bf16[4,2,2,40,1024]{4,3,2,0,1:T(8,128)(2,1)}, bf16[4,2,2,40,1024]{4,3,2,0,1:T(8,128)(2,1)}, u32[]{:S(2)}, u32[]{:S(2)}) collective-permute-start(bf16[4,2,2,40,1024]{4,3,2,0,1:T(8,128)(2,1)} %get-tuple-element.96), channel_id=1, source_target_pairs={{0,1},{1,0},{2,3},{3,2},{4,5},{5,4},{6,7},{7,6},{8,9},{9,8},{10,11... | collective-permute-start | bytes 3932168 | tf_op jit(solution)/shard_map/ppermute | solution.py:440
  143.5 18.0 %collective-permute-start.38 = (bf16[4,2,64,704]{3,2,1,0:T(8,128)(2,1)}, bf16[4,2,64,704]{3,2,1,0:T(8,128)(2,1)}, u32[]{:S(2)}, u32[]{:S(2)}) collective-permute-start(bf16[4,2,64,704]{3,2,1,0:T(8,128)(2,1)} %get-tuple-element.85), channel_id=1, source_target_pairs={{0,16},{8,24},{16,0},{24,8},{1,17},{9,25},{17,1},{25,9},{2,18},{10... | collective-permute-start | bytes 2162696 | tf_op jit(solution)/shard_map/ppermute | solution.py:443
  143.9 18.8 %collective-permute-start.34 = (bf16[4,2,64,704]{3,2,1,0:T(8,128)(2,1)}, bf16[4,2,64,704]{3,2,1,0:T(8,128)(2,1)}, u32[]{:S(2)}, u32[]{:S(2)}) collective-permute-start(bf16[4,2,64,704]{3,2,1,0:T(8,128)(2,1)} %get-tuple-element.86), channel_id=1, source_target_pairs={{0,8},{8,0},{16,24},{24,16},{1,9},{9,1},{17,25},{25,17},{2,10},{10... | collective-permute-start | bytes 2162696 | tf_op jit(solution)/shard_map/ppermute | solution.py:443
  145.4 120.5 %collective-permute-start.37 = (bf16[4,2,64,704]{3,2,1,0:T(8,128)(2,1)}, bf16[4,2,64,704]{3,2,1,0:T(8,128)(2,1)}, u32[]{:S(2)}, u32[]{:S(2)}) collective-permute-start(bf16[4,2,64,704]{3,2,1,0:T(8,128)(2,1)} %get-tuple-element.85), channel_id=1, source_target_pairs={{0,8},{8,0},{16,24},{24,16},{1,9},{9,1},{17,25},{25,17},{2,10},{10... | collective-permute-start | bytes 2162696 | tf_op jit(solution)/shard_map/ppermute | solution.py:443
  145.9 122.0 %collective-permute-start.35 = (bf16[4,2,64,704]{3,2,1,0:T(8,128)(2,1)}, bf16[4,2,64,704]{3,2,1,0:T(8,128)(2,1)}, u32[]{:S(2)}, u32[]{:S(2)}) collective-permute-start(bf16[4,2,64,704]{3,2,1,0:T(8,128)(2,1)} %get-tuple-element.86), channel_id=1, source_target_pairs={{0,16},{8,24},{16,0},{24,8},{1,17},{9,25},{17,1},{25,9},{2,18},{10... | collective-permute-start | bytes 2162696 | tf_op jit(solution)/shard_map/ppermute | solution.py:443
  161.5 104.4 %collective-permute-start.39 = (bf16[4,2,64,704]{3,2,1,0:T(8,128)(2,1)}, bf16[4,2,64,704]{3,2,1,0:T(8,128)(2,1)}, u32[]{:S(2)}, u32[]{:S(2)}) collective-permute-start(bf16[4,2,64,704]{3,2,1,0:T(8,128)(2,1)} %collective-permute-done.38), channel_id=1, source_target_pairs={{0,8},{8,0},{16,24},{24,16},{1,9},{9,1},{17,25},{25,17},{2,10},{10... | collective-permute-start | bytes 2162696 | tf_op jit(solution)/shard_map/ppermute | solution.py:443
  162.7 105.2 %collective-permute-start.36 = (bf16[4,2,64,704]{3,2,1,0:T(8,128)(2,1)}, bf16[4,2,64,704]{3,2,1,0:T(8,128)(2,1)}, u32[]{:S(2)}, u32[]{:S(2)}) collective-permute-start(bf16[4,2,64,704]{3,2,1,0:T(8,128)(2,1)} %collective-permute-done.34), channel_id=1, source_target_pairs={{0,16},{8,24},{16,0},{24,8},{1,17},{9,25},{17,1},{25,9},{2,18},{10... | collective-permute-start | bytes 2162696 | tf_op jit(solution)/shard_map/ppermute | solution.py:443
  258.6 11.1 %collective-permute-start.30 = (bf16[4,48,2048]{2,1,0:T(8,128)(2,1)S(1)}, bf16[4,48,2048]{2,1,0:T(8,128)(2,1)S(1)}, u32[]{:S(2)}, u32[]{:S(2)}) collective-permute-start(bf16[4,48,2048]{2,1,0:T(8,128)(2,1)S(1)} %fusion.67), channel_id=1, source_target_pairs={{0,1},{1,0},{2,3},{3,2},{4,5},{5,4},{6,7},{7,6},{8,9},{9,8},{10,11... | collective-permute-start | bytes 2359304 | tf_op jit(solution)/shard_map/ppermute | solution.py:440
  271.7 12.4 %collective-permute-start.31 = (bf16[48,2048]{1,0:T(8,128)(2,1)}, bf16[48,2048]{1,0:T(8,128)(2,1)}, u32[]{:S(2)}, u32[]{:S(2)}) collective-permute-start(bf16[48,2048]{1,0:T(8,128)(2,1)} %get-tuple-element.106), channel_id=1, source_target_pairs={{0,2},{1,3},{2,0},{3,1},{4,6},{5,7},{6,4},{7,5},{8,10},{9,11},{10,... | collective-permute-start | bytes 589832 | tf_op jit(solution)/shard_map/ppermute | solution.py:440
  271.7 12.4 %collective-permute-start.33 = (bf16[48,2048]{1,0:T(8,128)(2,1)}, bf16[48,2048]{1,0:T(8,128)(2,1)}, u32[]{:S(2)}, u32[]{:S(2)}) collective-permute-start(bf16[48,2048]{1,0:T(8,128)(2,1)} %get-tuple-element.107), channel_id=1, source_target_pairs={{0,6},{1,7},{2,4},{3,5},{4,2},{5,3},{6,0},{7,1},{8,14},{9,15},{10,... | collective-permute-start | bytes 589832 | tf_op jit(solution)/shard_map/ppermute | solution.py:440
  271.8 19.4 %collective-permute-start.32 = (bf16[48,2048]{1,0:T(8,128)(2,1)}, bf16[48,2048]{1,0:T(8,128)(2,1)}, u32[]{:S(2)}, u32[]{:S(2)}) collective-permute-start(bf16[48,2048]{1,0:T(8,128)(2,1)} %get-tuple-element.108), channel_id=1, source_target_pairs={{0,4},{1,5},{2,6},{3,7},{4,0},{5,1},{6,2},{7,3},{8,12},{9,13},{10,... | collective-permute-start | bytes 589832 | tf_op jit(solution)/shard_map/ppermute | solution.py:440
  294.4 139.8 %all-gather.11.cloned.1.call-start = ((), (), s32[]{:S(2)}) async-start(), calls=%async_computation.2 | async-start | bytes 1769472 | tf_op jit(solution)/shard_map/all_gather | solution.py:466
  356.8 26.9 %collective-permute-start.42 = (bf16[48,2048]{1,0:T(8,128)(2,1)S(1)}, bf16[48,2048]{1,0:T(8,128)(2,1)S(1)}, u32[]{:S(2)}, u32[]{:S(2)}) collective-permute-start(bf16[48,2048]{1,0:T(8,128)(2,1)S(1)} %get-tuple-element.105), channel_id=1, source_target_pairs={{0,4},{1,5},{2,6},{3,7},{4,0},{5,1},{6,2},{7,3},{8,12},{9,13},{10,... | collective-permute-start | bytes 589832 | tf_op jit(solution)/shard_map/ppermute | solution.py:440
  358.7 25.0 %collective-permute-start.45 = (bf16[48,2048]{1,0:T(8,128)(2,1)S(1)}, bf16[48,2048]{1,0:T(8,128)(2,1)S(1)}, u32[]{:S(2)}, u32[]{:S(2)}) collective-permute-start(bf16[48,2048]{1,0:T(8,128)(2,1)S(1)} %get-tuple-element.100), channel_id=1, source_target_pairs={{0,2},{1,3},{2,0},{3,1},{4,6},{5,7},{6,4},{7,5},{8,10},{9,11},{10,... | collective-permute-start | bytes 589832 | tf_op jit(solution)/shard_map/ppermute | solution.py:440
  359.7 24.0 %collective-permute-start.47 = (bf16[48,2048]{1,0:T(8,128)(2,1)S(1)}, bf16[48,2048]{1,0:T(8,128)(2,1)S(1)}, u32[]{:S(2)}, u32[]{:S(2)}) collective-permute-start(bf16[48,2048]{1,0:T(8,128)(2,1)S(1)} %get-tuple-element.101), channel_id=1, source_target_pairs={{0,6},{1,7},{2,4},{3,5},{4,2},{5,3},{6,0},{7,1},{8,14},{9,15},{10,... | collective-permute-start | bytes 589832 | tf_op jit(solution)/shard_map/ppermute | solution.py:440
  362.0 30.1 %collective-permute-start.46 = (bf16[48,2048]{1,0:T(8,128)(2,1)S(1)}, bf16[48,2048]{1,0:T(8,128)(2,1)S(1)}, u32[]{:S(2)}, u32[]{:S(2)}) collective-permute-start(bf16[48,2048]{1,0:T(8,128)(2,1)S(1)} %get-tuple-element.102), channel_id=1, source_target_pairs={{0,4},{1,5},{2,6},{3,7},{4,0},{5,1},{6,2},{7,3},{8,12},{9,13},{10,... | collective-permute-start | bytes 589832 | tf_op jit(solution)/shard_map/ppermute | solution.py:440
  397.1 179.2 %all-gather.9.cloned.1.call-start = ((), (), s32[]{:S(2)}) async-start(), calls=%async_computation.1 | async-start | bytes 1769472 | tf_op jit(solution)/shard_map/all_gather | solution.py:466
  433.9 177.5 %all-gather.15.cloned.1.call-start = ((), (), s32[]{:S(2)}) async-start(), calls=%async_computation.4 | async-start | bytes 1622016 | tf_op jit(solution)/shard_map/all_gather | solution.py:765
  518.7 14.7 %collective-permute-start.52 = (bf16[4,31,1024]{2,1,0:T(8,128)(2,1)S(1)}, bf16[4,31,1024]{2,1,0:T(8,128)(2,1)S(1)}, u32[]{:S(2)}, u32[]{:S(2)}) collective-permute-start(bf16[4,31,1024]{2,1,0:T(8,128)(2,1)S(1)} %fusion.111), channel_id=1, source_target_pairs={{0,1},{1,0},{2,3},{3,2},{4,5},{5,4},{6,7},{7,6},{8,9},{9,8},{10,11... | collective-permute-start | bytes 761864 | tf_op jit(solution)/shard_map/ppermute | solution.py:440
  550.3 87.1 %all-gather.13.cloned.1.call-start = ((), (), s32[]{:S(2)}) async-start(), calls=%async_computation.3 | async-start | bytes 1769472 | tf_op jit(solution)/shard_map/all_gather | solution.py:466
  554.2 18.8 %collective-permute-start.50 = (bf16[48,2048]{1,0:T(8,128)(2,1)S(1)}, bf16[48,2048]{1,0:T(8,128)(2,1)S(1)}, u32[]{:S(2)}, u32[]{:S(2)}) collective-permute-start(bf16[48,2048]{1,0:T(8,128)(2,1)S(1)} %get-tuple-element.99), channel_id=1, source_target_pairs={{0,4},{1,5},{2,6},{3,7},{4,0},{5,1},{6,2},{7,3},{8,12},{9,13},{10,... | collective-permute-start | bytes 589832 | tf_op jit(solution)/shard_map/ppermute | solution.py:440
  (201 other events, 2202.6 us)
Sparse Core Ops, SparseCore 0:
  294.5 24.5 all-gather.6
  397.2 24.8 all-gather.10
  434.0 26.7 all-gather.8
  550.4 60.8 all-gather.14
  613.4 23.8 all-gather.12
